TPU v7x, 256 devices: a whole 4x4x8 slice. The times are simulated.
256 devices in a mesh: dp: 32 (over z, y_hi, core), tensor: 8 (over y_lo, x).
Axes of the slice: x: 4, y: 4 (y_hi: 2, y_lo: 2; y = y_hi * 2 + y_lo), z: 8, core: 2. Of those that a mesh axis runs over, the one named last changes fastest.
Arguments:
- hidden: bfloat16 [16384, 8192], P(('dp', 'tensor')), may hold values from -6 to 6
- gain: float32 [8192], replicated, may hold values from 0.1 to 1.9
- segment_ids: int32 [32, 512], P('dp'), may hold values from 0 to 7, never falling along the last dimension, each value on 1 to 256 neighbouring positions
- w_query: bfloat16 [8192, 4096], P('dp', 'tensor'), may hold values from -1.5 to 1.5
- key_matrix: bfloat16 [8192, 1024], P('dp', 'tensor'), may hold values from -0.0625 to 0.0625
- value_matrix: bfloat16 [8192, 1024], P('dp', 'tensor'), may hold values from -0.0625 to 0.0625
- w_out: bfloat16 [4096, 8192], P('tensor', 'dp'), may hold values from -0.09375 to 0.09375
Outputs:
- attended: bfloat16 [16384, 8192], P(('dp', 'tensor'))
All inputs are finite; a program needn't handle non-finite values.
Results may differ from a plain program's by a relative error of at most 0.018.
Values may be sent and summed in bfloat16 or wider, within the bound.
A program may use at most 128 MiB of HBM per device.

v0:
```python
import math

import jax
import jax.numpy as jnp
from jax import lax
from jax.sharding import PartitionSpec as P

HEAD_SIZE = 128


def rms_norm(values, gain):
    expanded_heads = values.astype(jnp.float32)
    inv_rms = lax.rsqrt(jnp.mean(expanded_heads * expanded_heads, axis=-1, keepdims=True) + 1e-05)
    return (expanded_heads * inv_rms * gain).astype(jnp.bfloat16)


def seg_positions(segments):
    length = segments.shape[0]
    earlier = jnp.sum((segments[None, :] < segments[:, None]).astype(jnp.int32), axis=1)
    return (jnp.arange(length, dtype=jnp.int32) - earlier).astype(jnp.float32)


def apply_rotary(heads, token_places):
    half_width = heads.shape[-1] // 2
    freq_index = jnp.arange(half_width, dtype=jnp.float32)
    inverse = jnp.exp(freq_index * (-2.0 * math.log(500000.0) / heads.shape[-1]))
    angles = token_places[:, None] * inverse[None, :]
    cosine = jnp.cos(angles)[:, None, :]
    sine_part = jnp.sin(angles)[:, None, :]
    first_half = heads[..., :half_width]
    second = heads[..., half_width:]
    return jnp.concatenate(
        [first_half * cosine - second * sine_part, second * cosine + first_half * sine_part],
        axis=-1,
    )


def attend(query_heads, key_head_rows, value_head_rows, segments):
    length, kv_heads, head_width = key_head_rows.shape
    grouped = query_heads.reshape(length, kv_heads, -1, head_width)
    scores = jnp.einsum(
        "qkgd,skd->kgqs", grouped, key_head_rows, preferred_element_type=jnp.float32
    ) / math.sqrt(head_width)
    position_ids = jnp.arange(length, dtype=jnp.int32)
    allowed = (segments[:, None] == segments[None, :]) & (
        position_ids[None, :] <= position_ids[:, None]
    )
    scores = jnp.where(allowed, scores, jnp.float32(-1e30))
    row_max = jnp.max(scores, axis=-1, keepdims=True)
    exponent = jnp.exp(scores - row_max)
    weights = (exponent / jnp.sum(exponent, axis=-1, keepdims=True)).astype(jnp.bfloat16)
    mixed_heads = jnp.einsum(
        "kgqs,skd->qkgd", weights, value_head_rows, preferred_element_type=jnp.float32
    )
    return mixed_heads.reshape(length, -1).astype(jnp.bfloat16)


def body(hidden, gain, segment_ids, w_query, key_matrix, value_matrix, w_out):
    gathered = lax.all_gather(hidden, "tensor", axis=0, tiled=True)
    scaled_input = rms_norm(gathered, gain)
    length = scaled_input.shape[0]

    def add_rows(portion):
        return jnp.dot(scaled_input, portion, preferred_element_type=jnp.float32)

    key_sum = add_rows(lax.all_gather(key_matrix, "dp", axis=0, tiled=True))
    value_sum = add_rows(lax.all_gather(value_matrix, "dp", axis=0, tiled=True))
    query_sum = add_rows(lax.all_gather(w_query, "dp", axis=0, tiled=True))
    segments = segment_ids[0]
    token_places = seg_positions(segments)
    query_heads = apply_rotary(query_sum.reshape(length, -1, HEAD_SIZE), token_places).astype(
        jnp.bfloat16
    )
    key_head_rows = apply_rotary(key_sum.reshape(length, -1, HEAD_SIZE), token_places).astype(
        jnp.bfloat16
    )
    value_head_rows = value_sum.astype(jnp.bfloat16).reshape(length, -1, HEAD_SIZE)
    mixed_heads = attend(query_heads, key_head_rows, value_head_rows, segments)
    partial_value = jnp.dot(
        mixed_heads,
        lax.all_gather(w_out, "dp", axis=1, tiled=True),
        preferred_element_type=jnp.float32,
    )
    attended = lax.psum_scatter(
        partial_value.astype(jnp.bfloat16), "tensor", scatter_dimension=0, tiled=True
    )
    return attended


def solution(mesh):
    placed = (
        P(("dp", "tensor"), None),
        P(),
        P("dp", None),
        P("dp", "tensor"),
        P("dp", "tensor"),
        P("dp", "tensor"),
        P("tensor", "dp"),
    )
    return jax.shard_map(
        body, mesh=mesh, in_specs=placed, out_specs=P(("dp", "tensor"), None), check_vma=False
    )
```

profile of v0, /device:TPU:1, one launch (start us, length us, event | category | flops | bytes accessed | tf_op | source)
XLA Modules:
  0.0 585.1 jit_solution(12340822203435087897)
XLA Ops:
  6.5 0.7 all-gather.6.cloned.1.call-update
  7.3 0.0 all-gather.10.cloned.1.call-start
  7.3 0.7 all-gather.10.cloned.1.call-update
  8.0 0.0 all-gather.12.cloned.1.call-start
  8.1 0.7 all-gather.12.cloned.1.call-update
  8.7 0.0 all-gather.8.cloned.1.call-start
  8.8 0.5 all-gather.8.cloned.1.call-update
  9.3 0.0 all-gather.14.cloned.1.call-start
  9.4 0.5 all-gather.14.cloned.1.call-update
  9.9 0.0 reduce-scatter.2.cloned.1.call-start
  10.0 0.9 convert_reduce_fusion
  10.9 1.0 fusion.12
  11.9 1.0 multiply_cosine_fusion
  12.9 94.5 %all-gather.6.cloned.1.call-done = bf16[512,8192]{1,0:T(8,128)(2,1)} async-done(((bf16[64,8192]{1,0:T(8,128)(2,1)}), bf16[512,8192]{1,0:T(8,128)(2,1)}) %all-gather.6.cloned.1.call-update) | async-done | bytes 8388624 | tf_op jit(solution)/shard_map/all_gather | solution.py:59
  107.4 5.1 fusion
  112.5 76.9 %all-gather.10.cloned.1.call-done = bf16[8192,128]{1,0:T(8,128)(2,1)} async-done(((bf16[256,128]{1,0:T(8,128)(2,1)}), bf16[8192,128]{1,0:T(8,128)(2,1)}) %all-gather.10.cloned.1.call-update) | async-done | bytes 2097168 | tf_op jit(solution)/shard_map/all_gather | solution.py:66
  189.4 6.5 %convolution_bitcast_fusion = f32[512,1,128]{0,2,1:T(8,128)S(1)} fusion(bf16[8192,128]{1,0:T(8,128)(2,1)} %all-gather.10.cloned.1.call-done, bf16[512,8192]{1,0:T(8,128)(2,1)} %all-gather.6.cloned.1.call-done, f32[8192]{0:T(1024)S(1)} %copy-done.1, f32[512]{0:T(512)S(1)} %add_rsqrt_fusion), kind=kOutput, calls=%fused_computation.15 | convolution fusion | flops 1090519040 | bytes 10782720 | tf_op jit(solution)/shard_map/dot_general | solution.py:64
  195.9 0.6 fusion.28
  196.5 93.8 %all-gather.12.cloned.1.call-done = bf16[8192,512]{1,0:T(8,128)(2,1)} async-done(((bf16[256,512]{1,0:T(8,128)(2,1)}), bf16[8192,512]{1,0:T(8,128)(2,1)}) %all-gather.12.cloned.1.call-update) | async-done | bytes 8388624 | tf_op jit(solution)/shard_map/all_gather | solution.py:68
  290.3 11.5 %fusion.32 = f32[512,512]{0,1:T(8,128)S(1)} fusion(bf16[8192,512]{1,0:T(8,128)(2,1)} %all-gather.12.cloned.1.call-done, bf16[512,8192]{1,0:T(8,128)(2,1)} %all-gather.6.cloned.1.call-done, f32[8192]{0:T(1024)S(1)} %copy-done.1, f32[512]{0:T(512)S(1)} %add_rsqrt_fusion), kind=kOutput, calls=%fused_computation.50 | convolution fusion | flops 4311744512 | bytes 17860608 | tf_op jit(solution)/shard_map/dot_general | solution.py:64
  301.9 0.1 fusion.37
  301.9 0.3 copy.15
  302.3 0.3 copy.16
  302.6 0.3 subtract_convert_fusion
  302.9 1.2 fusion.4
  304.1 1.9 copy-done
  306.1 0.9 fusion.3
  307.0 62.4 %all-gather.8.cloned.1.call-done = bf16[8192,128]{1,0:T(8,128)(2,1)} async-done(((bf16[256,128]{1,0:T(8,128)(2,1)}), bf16[8192,128]{1,0:T(8,128)(2,1)}) %all-gather.8.cloned.1.call-update) | async-done | bytes 2097168 | tf_op jit(solution)/shard_map/all_gather | solution.py:67
  369.4 9.4 %fusion.8 = bf16[128,4,512]{2,0,1:T(8,128)(2,1)S(1)} fusion(f32[4,512]{1,0:T(4,128)S(1)} %fusion.3, f32[4,512]{1,0:T(4,128)S(1)} %get-tuple-element.13, f32[512,512,4]{1,0,2:T(8,128)} %copy-done, pred[512,512]{0,1:T(8,128)(4,1)S(1)} %fusion.12, bf16[8192,128]{1,0:T(8,128)(2,1)} %all-gather.8.cloned.1.call-done, ...), kind=kOutput, calls=%fused_computation.14 | convolution fusion | flops 1364525056 | bytes 15517696 | tf_op jit(solution)/shard_map/kgqs,skd->qkgd/dot_general | solution.py:52
  378.8 98.0 %all-gather.14.cloned.1.call-done = bf16[512,8192]{1,0:T(8,128)(2,1)} async-done(((bf16[512,256]{1,0:T(8,128)(2,1)}), bf16[512,8192]{1,0:T(8,128)(2,1)}) %all-gather.14.cloned.1.call-update) | async-done | bytes 8388624 | tf_op jit(solution)/shard_map/all_gather | solution.py:81
  476.8 10.1 %convolution_convert_fusion = bf16[512,8192]{1,0:T(8,128)(2,1)} fusion(bf16[512,512]{0,1:T(8,128)(2,1)S(1)} %bitcast.48, bf16[512,8192]{1,0:T(8,128)(2,1)} %all-gather.14.cloned.1.call-done), kind=kOutput, calls=%fused_computation.5 | convolution fusion | flops 4299161600 | bytes 17301504 | tf_op jit(solution)/shard_map/dot_general | solution.py:79
  486.9 91.3 %reduce-scatter.2.cloned.1.call-done = bf16[64,8192]{1,0:T(8,128)(2,1)} async-done(((bf16[512,8192]{1,0:T(8,128)(2,1)}), bf16[64,8192]{1,0:T(8,128)(2,1)}) %reduce-scatter.2.cloned.1.call-update) | async-done | bytes 1048592 | tf_op jit(solution)/shard_map/reduce_scatter | solution.py:84
  (10 shorter events, 0.1 us)
Async XLA Ops:
  6.5 182.9 %copy-start.1 = (f32[8192]{0:T(1024)S(1)}, f32[8192]{0:T(1024)}, u32[]{:S(2)}) copy-start(f32[8192]{0:T(1024)} %param.8) | copy-start | bytes 98308
  6.5 100.9 %all-gather.6.cloned.1.call-start = ((), (), s32[]{:S(2)}) async-start(), calls=%async_computation.1 | async-start | bytes 9437184 | tf_op jit(solution)/shard_map/all_gather | solution.py:59
  7.3 182.2 %all-gather.10.cloned.1.call-start = ((), (), s32[]{:S(2)}) async-start(), calls=%async_computation.3 | async-start | bytes 2162688 | tf_op jit(solution)/shard_map/all_gather | solution.py:66
  8.0 282.3 %all-gather.12.cloned.1.call-start = ((), (), s32[]{:S(2)}) async-start(), calls=%async_computation.4 | async-start | bytes 8650752 | tf_op jit(solution)/shard_map/all_gather | solution.py:68
  8.7 360.7 %all-gather.8.cloned.1.call-start = ((), (), s32[]{:S(2)}) async-start(), calls=%async_computation.2 | async-start | bytes 2162688 | tf_op jit(solution)/shard_map/all_gather | solution.py:67
  9.3 467.5 %all-gather.14.cloned.1.call-start = ((), (), s32[]{:S(2)}) async-start(), calls=%async_computation.5 | async-start | bytes 8650752 | tf_op jit(solution)/shard_map/all_gather | solution.py:81
  9.9 568.3 %reduce-scatter.2.cloned.1.call-start = ((), (), s32[]{:S(2)}) async-start(), calls=%async_computation.6 | async-start | bytes 9437184 | tf_op jit(solution)/shard_map/reduce_scatter | solution.py:84
  302.6 66.8 %copy-start.2 = (f32[8192]{0:T(1024)S(1)}, f32[8192]{0:T(1024)}, u32[]{:S(2)}) copy-start(f32[8192]{0:T(1024)} %param.8) | copy-start | bytes 98308
  304.1 1.9 copy-start
Sparse Core Ops, SparseCore 0:
  9.1 98.2 all-gather.5
  110.2 79.1 all-gather.9
  192.2 98.0 all-gather.11
  292.9 76.4 all-gather.7
  371.8 104.9 all-gather.13
  487.1 91.1 reduce-scatter.1
where the time goes:
time: 585 us
  waiting for transfers between devices  520 us (89%)
  matrix products  38.7 us (7%)
  between operations  13.6 us (2%)
  other arithmetic  9.75 us (2%)
    all_gather x1, waiting for transfers between devices, body(): lax.all_gather(w_out, 'dp', axis=1, tiled=True)  98 us
    all_gather x1, waiting for transfers between devices, body(): gathered = lax.all_gather(hidden, 'tensor', axis=0, tiled=True)  94.5 us
    all_gather x1, waiting for transfers between devices, body(): query_sum = add_rows(lax.all_gather(w_query, 'dp', axis=0, tiled=True))  93.8 us
    reduce_scatter x1, waiting for transfers between devices, body(): lax.psum_scatter(partial_value.astype(jnp.bfloat16), 'tensor', scatter_di...  91.3 us
    all_gather x1, waiting for transfers between devices, body(): key_sum = add_rows(lax.all_gather(key_matrix, 'dp', axis=0, tiled=True))  76.9 us
    all_gather x1, waiting for transfers between devices, body(): value_sum = add_rows(lax.all_gather(value_matrix, 'dp', axis=0, tiled=True))  62.4 us
    dot_general x2, matrix products, add_rows(): return jnp.dot(scaled_input, portion, preferred_element_type=jnp.float32)  18 us
  transfers between devices with their start and end apart: 6, of which 6 were waited for; matrix products, arithmetic and copies ran while one was open for 7% of the time, Pallas kernels for 0%

commit v1 on v0

v1 whole, which is shorter than its diff:
```python
import functools
import math

import jax
import jax.numpy as jnp
from jax import lax
from jax.experimental import pallas as pl
from jax.experimental.pallas import tpu as pltpu
from jax.sharding import PartitionSpec as P

MESH = pl.DeviceIdType.MESH
BF = jnp.bfloat16
F32 = jnp.float32
HEAD = 128
VMEM_LIMIT = 56 * 2**20

RELS = ((0, 0), (1, 1), (1, 0), (0, 1))
SLOT = {r: i for i, r in enumerate(RELS)}


def place():
    dp = lax.axis_index("dp")
    t = lax.axis_index("tensor")
    return t % 4, (dp // 2) % 2, t // 4, dp // 4, dp % 2


def device(x, yh, yl, z, k):
    return (z * 4 + yh * 2 + k, yl * 4 + x)


def flip(v, f):
    return 1 - v if f else v


class Copies:
    def __init__(self, send, recv):
        self.send, self.recv, self.n, self.open = send, recv, 0, []

    def to(self, src, dst, dev):
        i = self.n
        self.n += 1
        return pltpu.make_async_remote_copy(
            src_ref=src, dst_ref=dst, send_sem=self.send.at[i], recv_sem=self.recv.at[i],
            device_id=dev, device_id_type=MESH)

    def go(self, src, dst, dev):
        cp = self.to(src, dst, dev)
        cp.start()
        self.open.append(cp)
        return cp

    def finish(self):
        for cp in self.open:
            cp.wait_send()


N_A = 80


def project_kernel(hid, gain, wq, wk, wv, wo, tab,
                   qkv, tab_out, wo_all,
                   xn, xs, wa, wb, part, got, tab_in, send, recv, swap_send, swap_recv, got_sem):
    x, yh, yl, z, k = place()
    sib = device(x, yh, yl, z, 1 - k)
    swapped = device(x, yh, k, z, yl)
    cps = Copies(send, recv)

    def ydev(r):
        return device(x, flip(yh, r[0]), flip(yl, r[1]), z, k)

    def xdev(d):
        return device((x + d + 4) % 4, yh, yl, z, k)

    def zdev(d):
        return device(x, yh, yl, (z + d + 8) % 8, k)

    bar = pltpu.get_barrier_semaphore()
    for dev in [ydev(r) for r in RELS[1:]] + [xdev(d) for d in (1, 2, 3)] + [zdev(1), zdev(-1), sib]:
        pl.semaphore_signal(bar, inc=1, device_id=dev, device_id_type=MESH)

    @pl.when(k != yl)
    def _():
        pl.semaphore_signal(bar, inc=1, device_id=swapped, device_id_type=MESH)

    pl.semaphore_wait(bar, 9 + (k + yl) % 2)

    rows = pl.ds(pl.multiple_of(z * 256, 256), 256)
    mine = [
        (wq, wa.at[rows, :]),
        (wk, wb.at[rows, pl.ds(0, 128)]),
        (wv, wb.at[rows, pl.ds(128, 128)]),
        (wo, wo_all.at[z, pl.ds(pl.multiple_of(k * 512, 512), 512), :]),
    ]
    theirs = [
        (wq, wa.at[rows, :]),
        (wk, wb.at[rows, pl.ds(0, 128)]),
        (wv, wb.at[rows, pl.ds(128, 128)]),
        (wo, wo_all.at[z, pl.ds(pl.multiple_of(yl * 512, 512), 512), :]),
    ]

    @pl.when(k != yl)
    def _():
        for i, (s, d) in enumerate(theirs):
            pltpu.make_async_remote_copy(
                src_ref=s, dst_ref=d, send_sem=swap_send.at[i], recv_sem=swap_recv.at[i],
                device_id=swapped, device_id_type=MESH).start()

    @pl.when(k == yl)
    def _():
        for i, (s, d) in enumerate(mine):
            pltpu.make_async_copy(s, d, swap_recv.at[i]).start()

    def wait_swap(i):
        s, d = mine[i]
        pltpu.make_async_copy(s, d, swap_recv.at[i]).wait()

    h = hid[...].astype(F32)
    inv = lax.rsqrt(jnp.mean(h * h, axis=-1, keepdims=True) + 1e-5)

    def slice_norm(r, store):
        yy = flip(yh, r[0]) * 2 + flip(yl, r[1])
        for zz in range(8):
            cols = pl.ds(pl.multiple_of((zz * 4 + yy) * 256, 256), 256)
            v = hid[:, cols].astype(F32) * inv * gain[:, cols]
            store(zz, v.astype(BF))

    for r in (1, 2, 3):
        def put(zz, v, r=r):
            xn[r - 1, :, zz * 256:(zz + 1) * 256] = v
        slice_norm(RELS[r], put)

    ysend = {}
    for r in (1, 2, 3):
        ysend[r] = cps.go(xn.at[r - 1], xs.at[r, k, x], ydev(RELS[r]))

    def put0(zz, v):
        xs[0, k, x, :, zz * 256:(zz + 1) * 256] = v
    slice_norm(RELS[0], put0)

    xgot = {}
    sibs = {}

    def spread(r):
        for d in (2, 1, 3):
            xgot[r, d] = cps.go(xs.at[r, k, x], xs.at[r, k, x], xdev(d))
        sibs[r, 0] = cps.go(xs.at[r, k, x], xs.at[r, k, x], sib)

    def spread_sib(r):
        for d in (1, 3, 2):
            xgot[r, d].wait_recv()
            src = xs.at[r, k, (x - d + 4) % 4]
            sibs[r, d] = cps.go(src, src, sib)

    def wait_sib(r):
        for d in (0, 1, 3, 2):
            sibs[r, d].wait_recv()

    spread(0)

    tab_cp = cps.go(tab, tab_in, sib)

    ring = {}

    def ring_step(name, at, s):
        for hf in (0, 1):
            for d in (1, -1):
                if s == 3 and hf != (0 if d == 1 else 1):
                    continue
                if s > 0:
                    ring[name, s - 1, hf, d].wait_recv()
                b = at((z - d * s + 8) % 8, hf)
                ring[name, s, hf, d] = cps.go(b, b, zdev(d))

    def ring_end(name):
        ring[name, 2, 1, 1].wait_recv()
        ring[name, 2, 0, -1].wait_recv()
        ring[name, 3, 0, 1].wait_recv()
        ring[name, 3, 1, -1].wait_recv()

    def at_a(b, hf):
        return wa.at[pl.ds(pl.multiple_of(b * 256 + hf * 128, 128), 128), :]

    def at_b(b, hf):
        return wb.at[pl.ds(pl.multiple_of(b * 256 + hf * 128, 128), 128), :]

    def at_o(b, hf):
        return wo_all.at[b, pl.ds(pl.multiple_of(k * 512 + hf * 256, 256), 256), :]

    def compute(r, w_ref, c0, width):
        def one(c, carry):
            lhs = xs[r, c].reshape(256, 2048)
            part[r, c, :, c0:c0 + width] = jnp.dot(
                lhs, w_ref[...], preferred_element_type=F32).astype(BF)
            return carry
        lax.fori_loop(0, 2, one, 0)
        a, b = RELS[r]
        for e in (1, 0):
            if (a, e) == (0, 0):
                continue
            c = flip(yl, e)
            dst_rows = pl.ds(pl.multiple_of(flip(yl, b) * 256, 256), 256)
            slot = SLOT[(a, e)] - 1
            i = cps.n
            cps.n += 1
            cp = pltpu.make_async_remote_copy(
                src_ref=part.at[r, c, :, pl.ds(c0, width)],
                dst_ref=got.at[slot, dst_rows, pl.ds(c0, width)],
                send_sem=send.at[i], recv_sem=got_sem.at[slot],
                device_id=ydev((a, e)), device_id_type=MESH)
            cp.start()
            cps.open.append(cp)

    def comp_a(r):
        compute(r, wa, 0, 512)

    def comp_b(r):
        compute(r, wb, 512, 256)

    wait_swap(0)
    ring_step("a", at_a, 0)
    ring_step("a", at_a, 1)
    ysend[1].wait_recv()
    spread(1)
    ring_step("a", at_a, 2)
    wait_swap(1)
    wait_swap(2)
    ring_step("b", at_b, 0)
    ysend[2].wait_recv()
    spread(2)
    ysend[3].wait_recv()
    spread(3)
    ring_step("a", at_a, 3)
    ring_step("b", at_b, 1)
    spread_sib(0)
    ring_end("a")
    ring_step("b", at_b, 2)
    wait_sib(0)
    comp_a(0)
    wait_swap(3)
    ring_step("b", at_b, 3)
    ring_step("o", at_o, 0)
    spread_sib(1)
    wait_sib(1)
    comp_a(1)
    ring_end("b")
    comp_b(0)
    comp_b(1)
    ring_step("o", at_o, 1)
    spread_sib(2)
    wait_sib(2)
    comp_a(2)
    comp_b(2)
    ring_step("o", at_o, 2)
    spread_sib(3)
    wait_sib(3)
    comp_a(3)
    comp_b(3)
    ring_step("o", at_o, 3)

    tab_cp.wait_recv()
    keep = k == yl
    tab_out[...] = jnp.where(keep, tab[...], tab_in[...])
    ring_end("o")
    half = wo_all.at[:, pl.ds(pl.multiple_of(k * 512, 512), 512), :]
    wo_cp = cps.go(half, half, sib)

    for slot in range(3):
        pltpu.make_async_copy(got.at[slot], got.at[slot], got_sem.at[slot]).wait()
    for b in (0, 1):
        r = SLOT[(0, b)]
        rows_b = pl.ds(pl.multiple_of(flip(yl, b) * 256, 256), 256)
        total = part[r, yl].astype(F32)
        for slot in range(3):
            total += got[slot, rows_b, :].astype(F32)
        qkv[rows_b, :] = total
    wo_cp.wait_recv()

    @pl.when(k != yl)
    def _():
        for i, (s, d) in enumerate(theirs):
            pltpu.make_async_remote_copy(
                src_ref=s, dst_ref=d, send_sem=swap_send.at[i], recv_sem=swap_recv.at[i],
                device_id=swapped, device_id_type=MESH).wait_send()
    cps.finish()


def attend_kernel(qkv, tab, mixed):
    cos = tab[:, 0:128]
    sin = tab[:, 128:256]

    def rotate(u):
        return (u * cos + pltpu.roll(u, 64, axis=1) * sin).astype(BF)

    keys = rotate(qkv[:, 512:640])
    values = qkv[:, 640:768].astype(BF)
    queries = [rotate(qkv[:, i * 128:(i + 1) * 128]) for i in range(4)]
    scale = 1.0 / math.sqrt(HEAD)
    for i in range(4):
        lo, hi = i * 128, (i + 1) * 128
        q = jnp.concatenate([queries[j][lo:hi] for j in range(4)], axis=0)
        s = lax.dot_general(q, keys[:hi], (((1,), (1,)), ((), ())), preferred_element_type=F32) * scale
        where_i = lax.broadcasted_iota(jnp.int32, (128, hi), 0) + lo
        where_s = lax.broadcasted_iota(jnp.int32, (128, hi), 1)
        start = where_i - tab[lo:hi, 256:257].astype(jnp.int32)
        ok = (where_s <= where_i) & (where_s >= start)
        s = jnp.where(ok[None], s.reshape(4, 128, hi), -1e30)
        e = jnp.exp(s - jnp.max(s, axis=-1, keepdims=True))
        w = (e / jnp.sum(e, axis=-1, keepdims=True)).astype(BF)
        o = jnp.dot(w.reshape(512, hi), values[:hi], preferred_element_type=F32).astype(BF)
        for j in range(4):
            mixed[lo:hi, j * 128:(j + 1) * 128] = o[j * 128:(j + 1) * 128]


N_C = 40


def output_kernel(mixed, wo_all, out,
                  m, wo, part, rx, slab, ry, send, recv, m_send, m_recv, wo_sem):
    x, yh, yl, z, k = place()
    cps = Copies(send, recv)
    sib = device(x, yh, yl, z, 1 - k)

    def ydev(r):
        return device(x, flip(yh, r[0]), flip(yl, r[1]), z, k)

    def xdev(d):
        return device((x + d + 4) % 4, yh, yl, z, k)

    def mdev(r):
        return device(x, flip(yh, r[0]), flip(yl, r[1]), z, yl)

    wo_cp = pltpu.make_async_copy(wo_all, wo, wo_sem)
    wo_cp.start()

    bar = pltpu.get_barrier_semaphore()
    for dev in [ydev(r) for r in RELS[1:]] + [xdev(d) for d in (1, 2, 3)]:
        pl.semaphore_signal(bar, inc=1, device_id=dev, device_id_type=MESH)

    for a in (0, 1):
        for j in (0, 1):
            src = device(x, flip(yh, a), k, z, j)
            if a == 0:
                @pl.when((k != yl) | (k != j))
                def _():
                    pl.semaphore_signal(bar, inc=1, device_id=src, device_id_type=MESH)
            else:
                pl.semaphore_signal(bar, inc=1, device_id=src, device_id_type=MESH)
    pl.semaphore_wait(bar, 9 + (k + yl) % 2)

    order = (2, 1, 3, 0)
    sends = []
    for n, d in enumerate(order):
        xx = (x + d) % 4
        src = mixed.at[:, xx]
        dst = m.at[yh, :, xx, :, pl.ds(pl.multiple_of(k * 512, 512), 512)]
        for r in (2, 1, 3):
            cp = pltpu.make_async_remote_copy(
                src_ref=src, dst_ref=dst, send_sem=m_send.at[n, r], recv_sem=m_recv.at[n, yh, k],
                device_id=mdev(RELS[r]), device_id_type=MESH)
            cp.start()
            sends.append(cp)

        @pl.when(k == yl)
        def _():
            pltpu.make_async_copy(src, dst, m_recv.at[n, yh, k]).start()

        @pl.when(k != yl)
        def _():
            pltpu.make_async_remote_copy(
                src_ref=src, dst_ref=dst, send_sem=m_send.at[n, 0], recv_sem=m_recv.at[n, yh, k],
                device_id=sib, device_id_type=MESH).start()

    wo_cp.wait()
    got = {}
    for n, d in enumerate(order):
        xx = (x + d) % 4
        for a in (0, 1):
            for j in (0, 1):
                ref = m.at[a, :, xx, :, pl.ds(j * 512, 512)]
                pltpu.make_async_copy(ref, ref, m_recv.at[n, a, j]).wait()

        def one(zz, carry):
            lhs = m[:, :, xx].reshape(256, 1024)
            o = jnp.dot(lhs, wo[zz], preferred_element_type=F32).astype(BF)
            part[d, :, :, pl.ds(pl.multiple_of(zz * 256, 256), 256)] = o.reshape(4, 64, 256)
            return carry
        lax.fori_loop(0, 8, one, 0)
        if d:
            for r in (2, 1, 3, 0):
                yy = flip(yh, RELS[r][0]) * 2 + flip(yl, RELS[r][1])
                got[d, r] = cps.go(part.at[d, yy], rx.at[d - 1, r], xdev(d))

    ysend = {}
    y_self = yh * 2 + yl
    for r in (2, 1, 3, 0):
        yy = flip(yh, RELS[r][0]) * 2 + flip(yl, RELS[r][1])
        for d in (2, 1, 3):
            got[d, r].wait_recv()
        total = part[0, yy].astype(F32)
        for d in (1, 2, 3):
            total += rx[d - 1, r].astype(F32)
        total = total.astype(BF)
        if r:
            slab[r - 1] = total
            ysend[r] = cps.go(slab.at[r - 1], ry.at[r - 1], ydev(RELS[r]))
        else:
            for zz in range(8):
                out[:, pl.ds(pl.multiple_of((zz * 4 + y_self) * 256, 256), 256)] = total[:, zz * 256:(zz + 1) * 256]
    for r in (2, 1, 3):
        yy = flip(yh, RELS[r][0]) * 2 + flip(yl, RELS[r][1])
        ysend[r].wait_recv()
        for zz in range(8):
            out[:, pl.ds(pl.multiple_of((zz * 4 + yy) * 256, 256), 256)] = ry[r - 1, :, zz * 256:(zz + 1) * 256]

    for cp in sends:
        cp.wait_send()

    @pl.when(k != yl)
    def _():
        for n, d in enumerate(order):
            xx = (x + d) % 4
            pltpu.make_async_remote_copy(
                src_ref=mixed.at[:, xx], dst_ref=m.at[yh, :, xx, :, pl.ds(pl.multiple_of(k * 512, 512), 512)],
                send_sem=m_send.at[n, 0], recv_sem=m_recv.at[n, yh, k],
                device_id=sib, device_id_type=MESH).wait_send()
    cps.finish()


V = pl.BlockSpec(memory_space=pltpu.VMEM)
ANY = pl.BlockSpec(memory_space=pl.ANY)
DMA = pltpu.SemaphoreType.DMA


def tables(segments):
    length = segments.shape[0]
    earlier = jnp.sum((segments[None, :] < segments[:, None]).astype(jnp.int32), axis=1)
    pos = (jnp.arange(length, dtype=jnp.int32) - earlier).astype(F32)
    freq = jnp.arange(HEAD // 2, dtype=F32)
    inverse = jnp.exp(freq * (-2.0 * math.log(500000.0) / HEAD))
    angles = pos[:, None] * inverse[None, :]
    c, s = jnp.cos(angles), jnp.sin(angles)
    return jnp.concatenate([c, c, -s, s, jnp.broadcast_to(pos[:, None], (length, 128))], axis=1)


def body(hidden, gain, segment_ids, w_query, key_matrix, value_matrix, w_out):
    tab = tables(segment_ids[0])
    qkv, tab2, wo_all = pl.pallas_call(
        project_kernel,
        out_shape=(jax.ShapeDtypeStruct((512, 768), F32), jax.ShapeDtypeStruct((512, 384), F32),
                   jax.ShapeDtypeStruct((8, 1024, 256), BF)),
        in_specs=[V, V, ANY, ANY, ANY, ANY, V],
        out_specs=(V, V, ANY),
        scratch_shapes=[
            pltpu.VMEM((3, 64, 2048), BF),
            pltpu.VMEM((4, 2, 4, 64, 2048), BF),
            pltpu.VMEM((2048, 512), BF),
            pltpu.VMEM((2048, 256), BF),
            pltpu.VMEM((4, 2, 256, 768), BF),
            pltpu.VMEM((3, 512, 768), BF),
            pltpu.VMEM((512, 384), F32),
            DMA((N_A + 20,)), DMA((N_A + 20,)), DMA((4,)), DMA((4,)), DMA((3,)),
        ],
        compiler_params=pltpu.CompilerParams(
            collective_id=0, has_side_effects=True, vmem_limit_bytes=VMEM_LIMIT),
        name="project",
    )(hidden, gain.reshape(1, -1), w_query, key_matrix, value_matrix, w_out, tab)
    mixed = pl.pallas_call(
        attend_kernel,
        out_shape=jax.ShapeDtypeStruct((512, 512), BF),
        in_specs=[V, V],
        out_specs=V,
        compiler_params=pltpu.CompilerParams(vmem_limit_bytes=VMEM_LIMIT),
        name="attend",
    )(qkv, tab2)
    return pl.pallas_call(
        output_kernel,
        out_shape=jax.ShapeDtypeStruct((64, 8192), BF),
        in_specs=[V, ANY],
        out_specs=V,
        scratch_shapes=[
            pltpu.VMEM((2, 2, 4, 64, 1024), BF),
            pltpu.VMEM((8, 1024, 256), BF),
            pltpu.VMEM((4, 4, 64, 2048), BF),
            pltpu.VMEM((3, 4, 64, 2048), BF),
            pltpu.VMEM((3, 64, 2048), BF),
            pltpu.VMEM((3, 64, 2048), BF),
            DMA((N_C,)), DMA((N_C,)), DMA((4, 4)), DMA((4, 2, 2)), DMA,
        ],
        compiler_params=pltpu.CompilerParams(
            collective_id=1, has_side_effects=True, vmem_limit_bytes=VMEM_LIMIT),
        name="output",
    )(mixed.reshape(2, 4, 64, 512), wo_all)


def solution(mesh):
    placed = (
        P(("dp", "tensor"), None), P(), P("dp", None), P("dp", "tensor"),
        P("dp", "tensor"), P("dp", "tensor"), P("tensor", "dp"),
    )
    return jax.shard_map(
        body, mesh=mesh, in_specs=placed, out_specs=P(("dp", "tensor"), None), check_vma=False)
```

time: 585 us -> 161 us (0.28)
  waiting for transfers between devices: 520 us -> 0 us
  Pallas kernels: 0 us -> 155 us
  matrix products: 38.7 us -> 0 us
  between operations: 13.6 us -> 0.04 us
  other arithmetic: 9.75 us -> 2.02 us
    all_gather x5 -> x0, waiting for transfers between devices: 426 us -> none  [the longest x1 98 us: body(): lax.all_gather(w_out, 'dp', axis=1, tiled=True)]
    pallas_call x0 -> x3, Pallas kernels: none -> 155 us  [the longest x1 87.8 us: body(): pl.pallas_call(project_kernel, out_shape=(jax.ShapeDtypeStruct((512, 768)...]
    reduce_scatter x1 -> x0, waiting for transfers between devices: 91.3 us -> none  [body(): lax.psum_scatter(partial_value.astype(jnp.bfloat16), 'tensor', scatter_di...]
    dot_general x5 -> x0, matrix products: 38.7 us -> none  [the longest x2 18 us: add_rows(): return jnp.dot(scaled_input, portion, preferred_element_type=jnp.float32)]
    reduce_sum x3 -> x1, other arithmetic: 6.96 us -> 1.01 us  [tables(): jnp.sum((segments[None, :] < segments[:, None]).astype(jnp.int32), axis=1)]
  transfers between devices with their start and end apart: 6 -> 0, of which waited for: 6 -> 0; matrix products, arithmetic and copies ran while one was open for 7% -> 0% of each run, Pallas kernels for 0% -> 0%
where the time goes in v1:
time: 161 us
  Pallas kernels  155 us (96%)
  local copies, waits for them, and re-layouts  3.47 us (2%)
  other arithmetic  2.02 us (1%)
    pallas_call x1, Pallas kernels, body(): pl.pallas_call(project_kernel, out_shape=(jax.ShapeDtypeStruct((512, 768)...  87.8 us
    pallas_call x1, Pallas kernels, body(): pl.pallas_call(output_kernel, out_shape=jax.ShapeDtypeStruct((64, 8192),...  62.7 us
    pallas_call x1, Pallas kernels, body(): pl.pallas_call(attend_kernel, out_shape=jax.ShapeDtypeStruct((512, 512),...  4.61 us

profile of v1, /device:TPU:1, one launch (start us, length us, event | category | flops | bytes accessed | tf_op | source)
XLA Modules:
  0.0 160.7 jit_solution(18277023807567115543)
XLA Ops:
  0.0 1.0 convert_reduce_fusion
  1.0 0.1 broadcast_in_dim.2
  1.2 1.0 multiply_sine_fusion
  2.2 1.1 concatenate.3.tab
  3.2 87.8 %project.1 = (f32[512,768]{1,0:T(8,128)}, f32[512,384]{1,0:T(8,128)}, bf16[8,1024,256]{2,1,0:T(8,128)(2,1)}) custom-call(bf16[64,8192]{1,0:T(8,128)(2,1)} %hid.1, f32[1,8192]{1,0:T(1,128)} %bitcast.4, bf16[256,512]{1,0:T(8,128)(2,1)} %wq.1, bf16[256,128]{1,0:T(8,128)(2,1)} %wk.1, bf16[256,128]{1,0:T(8,128)(2,1)} %wv.1, bf16[512,256]{1,0:T(8,128)(2,1)} %wo.1, ...), custom_call_target="tpu_custom_call" | custom-call | tf_op jit(solution)/shard_map/project/pallas_call | solution.py:447
  91.1 4.6 %attend.1 = bf16[512,512]{1,0:T(8,128)(2,1)} custom-call(f32[512,768]{1,0:T(8,128)} %get-tuple-element.8.qkv, f32[512,384]{1,0:T(8,128)} %get-tuple-element.9.tab), custom_call_target="tpu_custom_call" | custom-call | tf_op jit(solution)/shard_map/attend/pallas_call | solution.py:467
  95.7 62.7 %output.1 = bf16[64,8192]{1,0:T(8,128)(2,1)} custom-call(bf16[2,4,64,512]{3,2,1,0:T(8,128)(2,1)} %bitcast.3, bf16[8,1024,256]{2,1,0:T(8,128)(2,1)} %get-tuple-element.10.wo_all), custom_call_target="tpu_custom_call" | custom-call | tf_op jit(solution)/shard_map/output/pallas_call | solution.py:475
  158.5 2.3 %copy.10 = bf16[64,8192]{1,0:T(8,128)(2,1)} copy(bf16[64,8192]{1,0:T(8,128)(2,1)} %output.1) | data formatting | bytes 2097152
  (2 shorter events, 0.0 us)

commit v2 on v0

v2 whole, which is shorter than its diff:
```python
import math

import jax
import jax.numpy as jnp
from jax import lax
from jax.experimental import pallas as pl
from jax.experimental.pallas import tpu as pltpu
from jax.sharding import PartitionSpec as P

MESH = pl.DeviceIdType.MESH
BF = jnp.bfloat16
F32 = jnp.float32
HEAD = 128
VMEM_LIMIT = 56 * 2**20

RELS = ((0, 0), (1, 1), (1, 0), (0, 1))
SLOT = {r: i for i, r in enumerate(RELS)}
N_COPIES = 240


def place():
    dp = lax.axis_index("dp")
    t = lax.axis_index("tensor")
    return t % 4, (dp // 2) % 2, t // 4, dp // 4, dp % 2


def device(x, yh, yl, z, k):
    return (z * 4 + yh * 2 + k, yl * 4 + x)


def flip(v, f):
    return 1 - v if f else v


def at(start, size):
    return pl.ds(pl.multiple_of(start, size), size)


class Copies:
    def __init__(self, send, recv):
        self.send, self.recv, self.n, self.open = send, recv, 0, []

    def go(self, src, dst, dev, recv=None):
        i = self.n
        self.n += 1
        cp = pltpu.make_async_remote_copy(
            src_ref=src, dst_ref=dst, send_sem=self.send.at[i],
            recv_sem=self.recv.at[i] if recv is None else recv,
            device_id=dev, device_id_type=MESH)
        cp.start()
        self.open.append(cp)
        return cp

    def finish(self):
        for cp in self.open:
            cp.wait_send()


def kernel(hid_in, gain, seg, wq, wk, wv, wo_in, out,
           hid, xn, xs, w, wo, part, got, segs, qs, ks, vs, mixed, m, part2, fwd, rx, slab, ry,
           send, recv, hid_sem, swap_send, swap_recv, got_sem, m_send, m_recv, fwd_sem):
    x, yh, yl, z, k = place()
    y_self = yh * 2 + yl
    sib = device(x, yh, yl, z, 1 - k)
    swapped = device(x, yh, k, z, yl)
    cps = Copies(send, recv)

    def ydev(r):
        return device(x, flip(yh, r[0]), flip(yl, r[1]), z, k)

    def xdev(d):
        return device((x + d + 4) % 4, yh, yl, z, k)

    def zdev(d):
        return device(x, yh, yl, (z + d + 8) % 8, k)

    def mdev(r):
        return device(x, flip(yh, r[0]), flip(yl, r[1]), z, yl)

    hid_cp = pltpu.make_async_copy(hid_in, hid, hid_sem)
    hid_cp.start()

    bar = pltpu.get_barrier_semaphore()
    for dev in [ydev(r) for r in RELS[1:]] + [xdev(1), xdev(-1), zdev(1), zdev(-1), sib]:
        pl.semaphore_signal(bar, inc=1, device_id=dev, device_id_type=MESH)

    @pl.when(k != yl)
    def _():
        pl.semaphore_signal(bar, inc=1, device_id=swapped, device_id_type=MESH)

    for a in (0, 1):
        for j in (0, 1):
            src = device(x, flip(yh, a), k, z, j)
            if a == 0:
                @pl.when((k != yl) | (k != j))
                def _():
                    pl.semaphore_signal(bar, inc=1, device_id=src, device_id_type=MESH)
            else:
                pl.semaphore_signal(bar, inc=1, device_id=src, device_id_type=MESH)
    pl.semaphore_wait(bar, 11 + 2 * ((k + yl) % 2))

    rows = at(z * 256, 256)
    pieces = [
        (wk, w.at[0, rows, pl.ds(0, 128)]),
        (wv, w.at[0, rows, pl.ds(128, 128)]),
        (wq.at[:, pl.ds(0, 256)], w.at[1, rows, :]),
        (wq.at[:, pl.ds(256, 256)], w.at[2, rows, :]),
    ]
    wo_mine = wo.at[z, at(k * 512, 512), :]
    wo_theirs = wo.at[z, at(yl * 512, 512), :]

    def swap_copy(i):
        src, dst = pieces[i] if i < 4 else (wo_in, wo_theirs)
        return pltpu.make_async_remote_copy(
            src_ref=src, dst_ref=dst, send_sem=swap_send.at[i], recv_sem=swap_recv.at[i],
            device_id=swapped, device_id_type=MESH)

    def own_copy(i):
        src, dst = pieces[i] if i < 4 else (wo_in, wo_mine)
        return pltpu.make_async_copy(src, dst, swap_recv.at[i])

    def swap(*which):
        @pl.when(k != yl)
        def _():
            for i in which:
                swap_copy(i).start()

        @pl.when(k == yl)
        def _():
            for i in which:
                own_copy(i).start()

    def wait_swap(*which):
        for i in which:
            own_copy(i).wait()

    swap(0, 1)

    hid_cp.wait()
    total = jnp.zeros((64, 256), F32)
    for i in range(32):
        v = hid[:, i * 256:(i + 1) * 256].astype(F32)
        total += v * v
    inv = lax.rsqrt(jnp.sum(total, axis=-1, keepdims=True) * (1.0 / 8192) + 1e-5)

    def slice_norm(r, store):
        yy = flip(yh, r[0]) * 2 + flip(yl, r[1])
        for zz in range(8):
            cols = at((zz * 4 + yy) * 256, 256)
            store(zz, (hid[:, cols].astype(F32) * inv * gain[:, cols]).astype(BF))

    def put0(zz, v):
        xs[0, k, x, :, zz * 256:(zz + 1) * 256] = v
    slice_norm(RELS[0], put0)

    xg, xh, sibs, ysend = {}, {}, {}, {}

    def to_sib(r, d):
        ref = xs.at[r, k, (x - d + 4) % 4]
        sibs[r, d] = cps.go(ref, ref, sib)

    def spread(r):
        if r:
            ysend[r].wait_recv()
        ref = xs.at[r, k, x]
        for d in (1, -1):
            xg[r, d] = cps.go(ref, ref, xdev(d))
        to_sib(r, 0)

    def relay(r):
        for d in (1, -1):
            xg[r, d].wait_recv()
            ref = xs.at[r, k, (x - d + 4) % 4, pl.ds(0 if d == 1 else 32, 32)]
            xh[r, d] = cps.go(ref, ref, xdev(d))
            to_sib(r, d)

    def last(r):
        xh[r, 1].wait_recv()
        xh[r, -1].wait_recv()
        to_sib(r, 2)

    ring = {}

    def ring_ref(n, b, hf):
        if n < 3:
            return w.at[n, at(b * 256 + hf * 128, 128), :]
        return wo.at[b, at(k * 512 + hf * 256, 256), :]

    def share(b):
        ref = wo.at[b, at(k * 512, 512), :]
        shared.append(cps.go(ref, ref, sib))

    shared = []

    def ring_step(n, s):
        for hf in (0, 1):
            for d in (1, -1):
                if s > 0:
                    ring[n, s - 1, hf, d].wait_recv()
                if s == 3 and hf != (0 if d == 1 else 1):
                    continue
                ref = ring_ref(n, (z - d * s + 8) % 8, hf)
                ring[n, s, hf, d] = cps.go(ref, ref, zdev(d))
        if n == 3:
            share((z + s) % 8)
            if s:
                share((z - s + 8) % 8)

    def ring_end(n):
        ring[n, 3, 0, 1].wait_recv()
        ring[n, 3, 1, -1].wait_recv()
        if n == 3:
            share((z + 4) % 8)

    def scatter(r, rows_at, size, c0, width):
        a, b = RELS[r]
        for e in (1, 0):
            if (a, e) == (0, 0):
                continue
            slot = SLOT[(a, e)] - 1
            cps.go(part.at[r, flip(yl, e), rows_at, pl.ds(c0, width)],
                   got.at[slot, at(flip(yl, b) * 256 + rows_at.start, size), pl.ds(c0, width)],
                   ydev((a, e)), recv=got_sem.at[slot])

    def comp(r, g):
        def one(c, carry):
            part[r, c, :, g * 256:(g + 1) * 256] = jnp.dot(
                xs[r, c].reshape(256, 2048), w[g], preferred_element_type=F32).astype(BF)
            return carry
        lax.fori_loop(0, 2, one, 0)
        scatter(r, pl.ds(0, 256), 256, g * 256, 256)

    def comp_slab(r, d):
        xx = (x - d + 4) % 4
        lhs = xs[r, :, xx].reshape(128, 2048)

        def one(g, carry):
            o = jnp.dot(lhs, w[g], preferred_element_type=F32).astype(BF)
            part[r, :, at(xx * 64, 64), at(g * 256, 256)] = o.reshape(2, 64, 256)
            return carry
        lax.fori_loop(0, 3, one, 0)
        scatter(r, at(xx * 64, 64), 64, 0, 768)

    spread(0)
    wait_swap(0, 1)
    ring_step(0, 0)
    swap(2)
    for r in (1, 2, 3):
        def put(zz, v, r=r):
            xn[r - 1, :, zz * 256:(zz + 1) * 256] = v
        slice_norm(RELS[r], put)
        ysend[r] = cps.go(xn.at[r - 1], xs.at[r, k, x], ydev(RELS[r]))
    swap(3, 4)
    segs[0] = jnp.broadcast_to(seg[...].astype(F32), (8, 512))
    seg_cp = cps.go(segs.at[0], segs.at[1], sib)
    ring_step(0, 1)
    relay(0)
    ring_step(0, 2)
    spread(1)
    wait_swap(2)
    ring_step(1, 0)
    ring_step(0, 3)
    last(0)
    ring_end(0)
    ring_step(1, 1)
    for d in (0, 1, -1, 2):
        sibs[0, d].wait_recv()
    comp(0, 0)
    spread(2)
    relay(1)
    ring_step(1, 2)
    wait_swap(3)
    ring_step(2, 0)
    ring_step(1, 3)

    seg_cp.wait_recv()
    own_row = jnp.where(k == yl, segs[0, 0:1, :], segs[1, 0:1, :])
    i_col = lax.broadcasted_iota(jnp.int32, (512, 512), 0)
    i_row = lax.broadcasted_iota(jnp.int32, (512, 512), 1)
    seg_col = jnp.sum(jnp.where(i_col == i_row, own_row, 0.0), axis=1, keepdims=True)
    start = jnp.sum(jnp.where(own_row < seg_col, 1.0, 0.0), axis=1, keepdims=True)
    lane = lax.broadcasted_iota(jnp.int32, (1, HEAD), 1)
    freq = jnp.where(lane < 64, lane, lane - 64).astype(F32)
    inverse = jnp.exp(freq * (-2.0 * math.log(500000.0) / HEAD))
    pos = lax.broadcasted_iota(jnp.int32, (512, 1), 0).astype(F32) - start
    angles = pos * inverse
    cos = jnp.cos(angles)
    sin = jnp.where(lane < 64, -1.0, 1.0) * jnp.sin(angles)

    last(1)
    for d in (0, 1, -1, 2):
        sibs[1, d].wait_recv()
    comp(1, 0)
    ring_end(1)
    comp(0, 1)
    comp(1, 1)
    ring_step(2, 1)
    spread(3)
    relay(2)
    ring_step(2, 2)
    wait_swap(4)
    ring_step(3, 0)
    ring_step(2, 3)
    last(2)
    for d in (0, 1, -1, 2):
        sibs[2, d].wait_recv()
    comp(2, 0)
    comp(2, 1)
    ring_end(2)
    comp(2, 2)
    comp(1, 2)
    comp(0, 2)
    ring_step(3, 1)
    relay(3)
    for d in (0, 1, -1):
        sibs[3, d].wait_recv()
        comp_slab(3, d)
    ring_step(3, 2)
    last(3)
    sibs[3, 2].wait_recv()
    comp_slab(3, 2)
    ring_step(3, 3)

    def rotate(u):
        return (u * cos_b + pltpu.roll(u, 64, axis=1) * sin_b).astype(BF)

    for slot in range(3):
        pltpu.make_async_copy(got.at[slot], got.at[slot], got_sem.at[slot]).wait()
    for b in (0, 1):
        r = SLOT[(0, b)]
        half = flip(yl, b)
        rows_b = at(half * 256, 256)
        cos_b = jnp.where(half == 0, cos[0:256], cos[256:512])
        sin_b = jnp.where(half == 0, sin[0:256], sin[256:512])
        for i in range(6):
            cols = slice(i * 128, (i + 1) * 128)
            u = part[r, yl, :, cols].astype(F32)
            for slot in range(3):
                u += got[slot, rows_b, cols].astype(F32)
            if i == 0:
                ks[rows_b, :] = rotate(u)
            elif i == 1:
                vs[rows_b, :] = u.astype(BF)
            else:
                qs[rows_b, (i - 2) * 128:(i - 1) * 128] = rotate(u)

    scale = 1.0 / math.sqrt(HEAD)

    def attend(i):
        lo, hi = i * 128, (i + 1) * 128
        q = jnp.concatenate([qs[lo:hi, j * 128:(j + 1) * 128] for j in range(4)], axis=0)
        s = lax.dot_general(q, ks[:hi], (((1,), (1,)), ((), ())), preferred_element_type=F32) * scale
        where_i = lax.broadcasted_iota(jnp.int32, (128, hi), 0) + lo
        where_s = lax.broadcasted_iota(jnp.int32, (128, hi), 1)
        ok = (where_s <= where_i) & (where_s >= start[lo:hi].astype(jnp.int32))
        s = jnp.where(ok[None], s.reshape(4, 128, hi), -1e30)
        e = jnp.exp(s - jnp.max(s, axis=-1, keepdims=True))
        weights = (e / jnp.sum(e, axis=-1, keepdims=True)).astype(BF)
        o = jnp.dot(weights.reshape(512, hi), vs[:hi], preferred_element_type=F32).astype(BF)
        for j in range(4):
            for half in (0, 1):
                mixed[i // 2, (i % 2) * 2 + half, :, j * 128:(j + 1) * 128] = (
                    o[j * 128 + half * 64:j * 128 + half * 64 + 64])

    order = ((2, 0), (2, 1), (1, 0), (3, 0), (1, 1), (3, 1), (0, 0), (0, 1))

    def mixed_refs(n):
        d, l = order[n]
        xx = (x + d) % 4
        return mixed.at[l, xx], m.at[yh, l, xx, :, at(k * 512, 512)]

    def mixed_sib(n):
        src, dst = mixed_refs(n)
        return pltpu.make_async_remote_copy(
            src_ref=src, dst_ref=dst, send_sem=m_send.at[n], recv_sem=m_recv.at[n, yh, k],
            device_id=sib, device_id_type=MESH)

    def send_mixed(n):
        src, dst = mixed_refs(n)
        for r in (2, 1, 3):
            cps.go(src, dst, mdev(RELS[r]), recv=m_recv.at[n, yh, k])

        @pl.when(k == yl)
        def _():
            pltpu.make_async_copy(src, dst, m_recv.at[n, yh, k]).start()

        @pl.when(k != yl)
        def _():
            mixed_sib(n).start()

    attend(0)
    attend(1)
    send_mixed(0)
    attend(2)
    attend(3)
    for n in range(1, 8):
        send_mixed(n)
    ring_end(3)
    for cp in shared:
        cp.wait_recv()

    lo_cols, hi_cols = pl.ds(0, 1024), pl.ds(1024, 1024)

    def comp_out(n):
        d, l = order[n]
        xx = (x + d) % 4
        for a in (0, 1):
            for j in (0, 1):
                ref = m.at[a, l, xx, :, pl.ds(j * 512, 512)]
                pltpu.make_async_copy(ref, ref, m_recv.at[n, a, j]).wait()
        lhs = m[:, l, xx].reshape(128, 1024)

        def one(zz, carry):
            o = jnp.dot(lhs, wo[zz], preferred_element_type=F32).astype(BF)
            part2[d, :, l, :, at(zz * 256, 256)] = o.reshape(2, 64, 256)
            return carry
        lax.fori_loop(0, 8, one, 0)

    for n in (0, 1):
        comp_out(n)
        l = order[n][1]
        for a in (0, 1):
            cps.go(part2.at[2, a, l, :, hi_cols], fwd.at[0, a, l], xdev(1), recv=fwd_sem.at[0, a, l])
            cps.go(part2.at[2, a, l, :, lo_cols], fwd.at[1, a, l], xdev(-1), recv=fwd_sem.at[1, a, l])
    for n in range(2, 6):
        comp_out(n)

    alone, summed = {}, {}
    rel_order = (2, 1, 3, 0)

    def slab_at(r):
        return flip(yh, RELS[r][0]), flip(yl, RELS[r][1])

    for r in rel_order:
        a, l = slab_at(r)
        alone[r, 1] = cps.go(part2.at[1, a, l, :, lo_cols], rx.at[0, r, :, lo_cols], xdev(1))
        alone[r, -1] = cps.go(part2.at[3, a, l, :, hi_cols], rx.at[1, r, :, hi_cols], xdev(-1))
        for i, d, cols in ((0, 1, slice(1024, 2048)), (1, -1, slice(0, 1024))):
            ref = fwd.at[i, a, l]
            pltpu.make_async_copy(ref, ref, fwd_sem.at[i, a, l]).wait()
            part2[d % 4, a, l, :, cols] = (
                part2[d % 4, a, l, :, cols].astype(F32) + fwd[i, a, l].astype(F32)).astype(BF)
            pcols = pl.ds(cols.start, 1024)
            summed[r, d] = cps.go(part2.at[d % 4, a, l, :, pcols], rx.at[i, r, :, pcols], xdev(d))
    for n in (6, 7):
        comp_out(n)

    last_send = {}
    for r in rel_order:
        a, l = slab_at(r)
        for d in (1, -1):
            alone[r, d].wait_recv()
            summed[r, d].wait_recv()
        o = (part2[0, a, l].astype(F32) + rx[0, r].astype(F32) + rx[1, r].astype(F32)).astype(BF)
        if r:
            slab[r - 1] = o
            last_send[r] = cps.go(slab.at[r - 1], ry.at[r - 1], ydev(RELS[r]))
        else:
            for zz in range(8):
                out[:, at((zz * 4 + y_self) * 256, 256)] = o[:, zz * 256:(zz + 1) * 256]
    for r in (2, 1, 3):
        a, l = slab_at(r)
        last_send[r].wait_recv()
        for zz in range(8):
            out[:, at((zz * 4 + a * 2 + l) * 256, 256)] = ry[r - 1, :, zz * 256:(zz + 1) * 256]

    @pl.when(k != yl)
    def _():
        for i in range(5):
            swap_copy(i).wait_send()
        for n in range(8):
            mixed_sib(n).wait_send()
    cps.finish()


V = pl.BlockSpec(memory_space=pltpu.VMEM)
ANY = pl.BlockSpec(memory_space=pl.ANY)
DMA = pltpu.SemaphoreType.DMA


def body(hidden, gain, segment_ids, w_query, key_matrix, value_matrix, w_out):
    return pl.pallas_call(
        kernel,
        out_shape=jax.ShapeDtypeStruct((64, 8192), BF),
        in_specs=[ANY, V, V, ANY, ANY, ANY, ANY],
        out_specs=V,
        scratch_shapes=[
            pltpu.VMEM((64, 8192), BF),
            pltpu.VMEM((3, 64, 2048), BF),
            pltpu.VMEM((4, 2, 4, 64, 2048), BF),
            pltpu.VMEM((3, 2048, 256), BF),
            pltpu.VMEM((8, 1024, 256), BF),
            pltpu.VMEM((4, 2, 256, 768), BF),
            pltpu.VMEM((3, 512, 768), BF),
            pltpu.VMEM((2, 8, 512), F32),
            pltpu.VMEM((512, 512), BF),
            pltpu.VMEM((512, 128), BF),
            pltpu.VMEM((512, 128), BF),
            pltpu.VMEM((2, 4, 64, 512), BF),
            pltpu.VMEM((2, 2, 4, 64, 1024), BF),
            pltpu.VMEM((4, 2, 2, 64, 2048), BF),
            pltpu.VMEM((2, 2, 2, 64, 1024), BF),
            pltpu.VMEM((2, 4, 64, 2048), BF),
            pltpu.VMEM((3, 64, 2048), BF),
            pltpu.VMEM((3, 64, 2048), BF),
            DMA((N_COPIES,)), DMA((N_COPIES,)), DMA, DMA((5,)), DMA((5,)), DMA((3,)),
            DMA((8,)), DMA((8, 2, 2)), DMA((2, 2, 2)),
        ],
        compiler_params=pltpu.CompilerParams(
            collective_id=0, has_side_effects=True, vmem_limit_bytes=VMEM_LIMIT),
        name="sublayer",
    )(hidden, gain.reshape(1, -1), segment_ids, w_query, key_matrix, value_matrix, w_out)


def solution(mesh):
    placed = (
        P(("dp", "tensor"), None), P(), P("dp", None), P("dp", "tensor"),
        P("dp", "tensor"), P("dp", "tensor"), P("tensor", "dp"),
    )
    return jax.shard_map(
        body, mesh=mesh, in_specs=placed, out_specs=P(("dp", "tensor"), None), check_vma=False)
```

time: 585 us -> 140 us (0.24)
  waiting for transfers between devices: 520 us -> 0 us
  Pallas kernels: 0 us -> 136 us
  matrix products: 38.7 us -> 0 us
  between operations: 13.6 us -> 0.01 us
  other arithmetic: 9.75 us -> 0 us
    all_gather x5 -> x0, waiting for transfers between devices: 426 us -> none  [the longest x1 98 us: body(): lax.all_gather(w_out, 'dp', axis=1, tiled=True)]
    pallas_call x0 -> x1, Pallas kernels: none -> 136 us  [body(): pl.pallas_call(kernel, out_shape=jax.ShapeDtypeStruct((64, 8192), BF), in...]
    reduce_scatter x1 -> x0, waiting for transfers between devices: 91.3 us -> none  [body(): lax.psum_scatter(partial_value.astype(jnp.bfloat16), 'tensor', scatter_di...]
    dot_general x5 -> x0, matrix products: 38.7 us -> none  [the longest x2 18 us: add_rows(): return jnp.dot(scaled_input, portion, preferred_element_type=jnp.float32)]
    reduce_sum x3 -> x0, other arithmetic: 6.96 us -> none  [the longest x1 5.1 us: rms_norm(): jnp.mean(expanded_heads * expanded_heads, axis=-1, keepdims=True) + 1e-05]
  transfers between devices with their start and end apart: 6 -> 0, of which waited for: 6 -> 0; matrix products, arithmetic and copies ran while one was open for 7% -> 0% of each run, Pallas kernels for 0% -> 0%
where the time goes in v2:
time: 140 us; the launch traced here: 138 us
  Pallas kernels  136 us (97%)
  local copies, waits for them, and re-layouts  2.26 us (2%)
    pallas_call x1, Pallas kernels, body(): pl.pallas_call(kernel, out_shape=jax.ShapeDtypeStruct((64, 8192), BF), in...  136 us

profile of v2, /device:TPU:1, one launch (start us, length us, event | category | flops | bytes accessed | tf_op | source)
XLA Modules:
  0.0 138.1 jit_solution(17533864996420743376)
XLA Ops:
  0.0 135.8 %sublayer.1 = bf16[64,8192]{1,0:T(8,128)(2,1)} custom-call(bf16[64,8192]{1,0:T(8,128)(2,1)} %hid_in.1, f32[1,8192]{1,0:T(1,128)} %bitcast.1, s32[1,512]{1,0:T(1,128)} %seg.1, bf16[256,512]{1,0:T(8,128)(2,1)} %wq.1, bf16[256,128]{1,0:T(8,128)(2,1)} %wk.1, bf16[256,128]{1,0:T(8,128)(2,1)} %wv.1, bf16[512,256]{1,0:T(8,128)(2,1)} %wo_in.1), custom_call_target="tpu_custom_call" | custom-call | tf_op jit(solution)/shard_map/sublayer/pallas_call | solution.py:482
  135.8 2.3 %copy.9 = bf16[64,8192]{1,0:T(8,128)(2,1)} copy(bf16[64,8192]{1,0:T(8,128)(2,1)} %sublayer.1) | data formatting | bytes 2097152

commit v3 on v2

--- a/solution.py
+++ b/solution.py
@@ -57,7 +57,7 @@
 
 
 def kernel(hid_in, gain, seg, wq, wk, wv, wo_in, out,
-           hid, xn, xs, w, wo, part, got, segs, qs, ks, vs, mixed, m, part2, fwd, rx, slab, ry,
+           hid, xn, xs, w, wo, part, got, fa, fb, segs, qs, ks, vs, mixed, m, part2, fwd, rx, slab, ry,
            send, recv, hid_sem, swap_send, swap_recv, got_sem, m_send, m_recv, fwd_sem):
     x, yh, yl, z, k = place()
     y_self = yh * 2 + yl
@@ -119,7 +119,11 @@
         src, dst = pieces[i] if i < 4 else (wo_in, wo_mine)
         return pltpu.make_async_copy(src, dst, swap_recv.at[i])
 
-    def swap(*which):
+    groups = ((0, 1), (2,), (3,), (4,))
+
+    def swap(group):
+        which = groups[group]
+
         @pl.when(k != yl)
         def _():
             for i in which:
@@ -130,11 +134,11 @@
             for i in which:
                 own_copy(i).start()
 
-    def wait_swap(*which):
-        for i in which:
+    def wait_swap(group):
+        for i in groups[group]:
             own_copy(i).wait()
 
-    swap(0, 1)
+    swap(0)
 
     hid_cp.wait()
     total = jnp.zeros((64, 256), F32)
@@ -151,7 +155,11 @@
 
     def put0(zz, v):
         xs[0, k, x, :, zz * 256:(zz + 1) * 256] = v
-    slice_norm(RELS[0], put0)
+
+    def put_norm(r):
+        def put(zz, v):
+            xn[r - 1, :, zz * 256:(zz + 1) * 256] = v
+        slice_norm(RELS[r], put)
 
     xg, xh, sibs, ysend = {}, {}, {}, {}
 
@@ -167,12 +175,11 @@
             xg[r, d] = cps.go(ref, ref, xdev(d))
         to_sib(r, 0)
 
-    def relay(r):
-        for d in (1, -1):
-            xg[r, d].wait_recv()
-            ref = xs.at[r, k, (x - d + 4) % 4, pl.ds(0 if d == 1 else 32, 32)]
-            xh[r, d] = cps.go(ref, ref, xdev(d))
-            to_sib(r, d)
+    def relay(r, d):
+        xg[r, d].wait_recv()
+        ref = xs.at[r, k, (x - d + 4) % 4, pl.ds(0 if d == 1 else 32, 32)]
+        xh[r, d] = cps.go(ref, ref, xdev(d))
+        to_sib(r, d)
 
     def last(r):
         xh[r, 1].wait_recv()
@@ -192,19 +199,22 @@
 
     shared = []
 
-    def ring_step(n, s):
-        for hf in (0, 1):
-            for d in (1, -1):
-                if s > 0:
-                    ring[n, s - 1, hf, d].wait_recv()
-                if s == 3 and hf != (0 if d == 1 else 1):
-                    continue
-                ref = ring_ref(n, (z - d * s + 8) % 8, hf)
-                ring[n, s, hf, d] = cps.go(ref, ref, zdev(d))
-        if n == 3:
+    def ring_half(n, s, hf):
+        for d in (1, -1):
+            if s > 0:
+                ring[n, s - 1, hf, d].wait_recv()
+            if s == 3 and hf != (0 if d == 1 else 1):
+                continue
+            ref = ring_ref(n, (z - d * s + 8) % 8, hf)
+            ring[n, s, hf, d] = cps.go(ref, ref, zdev(d))
+        if n == 3 and hf == 1:
             share((z + s) % 8)
             if s:
                 share((z - s + 8) % 8)
+
+    def ring_step(n, s):
+        ring_half(n, s, 0)
+        ring_half(n, s, 1)
 
     def ring_end(n):
         ring[n, 3, 0, 1].wait_recv()
@@ -212,23 +222,31 @@
         if n == 3:
             share((z + 4) % 8)
 
-    def scatter(r, rows_at, size, c0, width):
+    far_a, far_b = {}, {}
+    near, pair = RELS[1], RELS[3]
+    low, high = pl.ds(0, 32), pl.ds(32, 32)
+
+    def send_sum(r, xx, half, cols):
         a, b = RELS[r]
-        for e in (1, 0):
-            if (a, e) == (0, 0):
-                continue
-            slot = SLOT[(a, e)] - 1
-            cps.go(part.at[r, flip(yl, e), rows_at, pl.ds(c0, width)],
-                   got.at[slot, at(flip(yl, b) * 256 + rows_at.start, size), pl.ds(c0, width)],
-                   ydev((a, e)), recv=got_sem.at[slot])
+        slot = 0 if a else 1
+        cps.go(part.at[r, 1 - yl, xx, half, cols], got.at[slot, flip(yl, b), xx, half, cols],
+               ydev(near if a else pair), recv=got_sem.at[slot])
 
     def comp(r, g):
+        a, b = RELS[r]
+        cols = pl.ds(g * 256, 256)
+
         def one(c, carry):
-            part[r, c, :, g * 256:(g + 1) * 256] = jnp.dot(
-                xs[r, c].reshape(256, 2048), w[g], preferred_element_type=F32).astype(BF)
+            o = jnp.dot(xs[r, c].reshape(256, 2048), w[g], preferred_element_type=F32)
+            part[r, c, :, :, g * 256:(g + 1) * 256] = o.astype(BF).reshape(4, 64, 256)
             return carry
         lax.fori_loop(0, 2, one, 0)
-        scatter(r, pl.ds(0, 256), 256, g * 256, 256)
+        if a:
+            far_a[b, g] = cps.go(part.at[r, yl, :, low, cols], fa.at[1 - b, :, :, cols], ydev(pair))
+            far_b[b, g] = cps.go(part.at[r, yl, :, high, cols], fb.at[1 - b, :, :, cols], ydev(near))
+            send_sum(r, slice(None), high, cols)
+        else:
+            send_sum(r, slice(None), low, cols)
 
     def comp_slab(r, d):
         xx = (x - d + 4) % 4
@@ -236,95 +254,165 @@
 
         def one(g, carry):
             o = jnp.dot(lhs, w[g], preferred_element_type=F32).astype(BF)
-            part[r, :, at(xx * 64, 64), at(g * 256, 256)] = o.reshape(2, 64, 256)
+            part[r, :, xx, :, at(g * 256, 256)] = o.reshape(2, 64, 256)
             return carry
         lax.fori_loop(0, 3, one, 0)
-        scatter(r, at(xx * 64, 64), 64, 0, 768)
-
+        send_sum(r, xx, low, slice(None))
+
+    folded = set()
+
+    def fold(r, i):
+        a, b = RELS[r]
+        far, buf, half, rows32 = (far_a, fa, low, slice(0, 32)) if a else (far_b, fb, high, slice(32, 64))
+        slabs = r == 3
+        for g in range(3) if slabs else (i,):
+            if (r, g) not in folded:
+                folded.add((r, g))
+                far[1 - b, g].wait_recv()
+        if slabs:
+            xx, cols = (x - i + 4) % 4, slice(0, 768)
+            part[r, 1 - yl, xx, rows32, cols] = (
+                part[r, 1 - yl, xx, rows32, cols].astype(F32) + buf[b, xx].astype(F32)).astype(BF)
+            send_sum(r, xx, half, slice(None))
+        else:
+            cols = slice(i * 256, (i + 1) * 256)
+            part[r, 1 - yl, :, rows32, cols] = (
+                part[r, 1 - yl, :, rows32, cols].astype(F32) + buf[b, :, :, cols].astype(F32)).astype(BF)
+            send_sum(r, slice(None), half, pl.ds(i * 256, 256))
+
+    def send_slice(r):
+        ysend[r] = cps.go(xn.at[r - 1], xs.at[r, k, x], ydev(RELS[r]))
+
+    def wait_sib(r):
+        for d in (0, 1, -1, 2):
+            sibs[r, d].wait_recv()
+
+    tab = {}
+
+    def tables():
+        seg_cp.wait_recv()
+        own_row = jnp.where(k == yl, segs[0, 0:1, :], segs[1, 0:1, :])
+        i_col = lax.broadcasted_iota(jnp.int32, (512, 512), 0)
+        i_row = lax.broadcasted_iota(jnp.int32, (512, 512), 1)
+        seg_col = jnp.sum(jnp.where(i_col == i_row, own_row, 0.0), axis=1, keepdims=True)
+        start = jnp.sum(jnp.where(own_row < seg_col, 1.0, 0.0), axis=1, keepdims=True)
+        lane = lax.broadcasted_iota(jnp.int32, (1, HEAD), 1)
+        freq = jnp.where(lane < 64, lane, lane - 64).astype(F32)
+        inverse = jnp.exp(freq * (-2.0 * math.log(500000.0) / HEAD))
+        pos = lax.broadcasted_iota(jnp.int32, (512, 1), 0).astype(F32) - start
+        angles = pos * inverse
+        cos = jnp.cos(angles)
+        sin = jnp.where(lane < 64, -1.0, 1.0) * jnp.sin(angles)
+        tab.update(start=start, cos=cos, sin=sin)
+
+    put_norm(1)
+    send_slice(1)
+    slice_norm(RELS[0], put0)
     spread(0)
-    wait_swap(0, 1)
-    ring_step(0, 0)
-    swap(2)
-    for r in (1, 2, 3):
-        def put(zz, v, r=r):
-            xn[r - 1, :, zz * 256:(zz + 1) * 256] = v
-        slice_norm(RELS[r], put)
-        ysend[r] = cps.go(xn.at[r - 1], xs.at[r, k, x], ydev(RELS[r]))
-    swap(3, 4)
+    swap(1)
+    put_norm(2)
+    put_norm(3)
     segs[0] = jnp.broadcast_to(seg[...].astype(F32), (8, 512))
     seg_cp = cps.go(segs.at[0], segs.at[1], sib)
-    ring_step(0, 1)
-    relay(0)
-    ring_step(0, 2)
+
+    wait_swap(0)
+    ring_half(0, 0, 0)
+    ring_half(0, 0, 1)
+    wait_swap(1)
+    ring_half(1, 0, 0)
+    ring_half(1, 0, 1)
+    swap(2)
+    ring_half(0, 1, 0)
     spread(1)
+    send_slice(2)
+    relay(0, -1)
+    relay(0, 1)
+    ring_half(0, 1, 1)
     wait_swap(2)
-    ring_step(1, 0)
-    ring_step(0, 3)
+    ring_half(2, 0, 0)
+    ring_half(2, 0, 1)
+    swap(3)
+    ring_half(1, 1, 0)
+    ring_half(1, 1, 1)
+    ring_half(0, 2, 0)
+    ring_half(0, 2, 1)
+    ring_half(2, 1, 0)
+    relay(1, -1)
+    relay(1, 1)
+    spread(2)
+    send_slice(3)
+    ring_half(2, 1, 1)
+    ring_half(1, 2, 0)
     last(0)
+    tables()
+    ring_half(1, 2, 1)
+    ring_half(0, 3, 0)
+    last(1)
+    ring_half(0, 3, 1)
+    ring_half(2, 2, 0)
+    spread(3)
+    ring_half(2, 2, 1)
+    ring_half(1, 3, 0)
+    relay(2, -1)
+    relay(2, 1)
+    ring_half(1, 3, 1)
+    wait_sib(1)
     ring_end(0)
-    ring_step(1, 1)
-    for d in (0, 1, -1, 2):
-        sibs[0, d].wait_recv()
+    comp(1, 0)
+    wait_sib(0)
     comp(0, 0)
-    spread(2)
-    relay(1)
-    ring_step(1, 2)
+    ring_half(2, 3, 0)
+    ring_half(2, 3, 1)
     wait_swap(3)
-    ring_step(2, 0)
-    ring_step(1, 3)
-
-    seg_cp.wait_recv()
-    own_row = jnp.where(k == yl, segs[0, 0:1, :], segs[1, 0:1, :])
-    i_col = lax.broadcasted_iota(jnp.int32, (512, 512), 0)
-    i_row = lax.broadcasted_iota(jnp.int32, (512, 512), 1)
-    seg_col = jnp.sum(jnp.where(i_col == i_row, own_row, 0.0), axis=1, keepdims=True)
-    start = jnp.sum(jnp.where(own_row < seg_col, 1.0, 0.0), axis=1, keepdims=True)
-    lane = lax.broadcasted_iota(jnp.int32, (1, HEAD), 1)
-    freq = jnp.where(lane < 64, lane, lane - 64).astype(F32)
-    inverse = jnp.exp(freq * (-2.0 * math.log(500000.0) / HEAD))
-    pos = lax.broadcasted_iota(jnp.int32, (512, 1), 0).astype(F32) - start
-    angles = pos * inverse
-    cos = jnp.cos(angles)
-    sin = jnp.where(lane < 64, -1.0, 1.0) * jnp.sin(angles)
-
-    last(1)
-    for d in (0, 1, -1, 2):
-        sibs[1, d].wait_recv()
-    comp(1, 0)
+    ring_half(3, 0, 0)
+    ring_half(3, 0, 1)
+    relay(3, -1)
+    relay(3, 1)
     ring_end(1)
+    comp(1, 1)
+    fold(0, 0)
     comp(0, 1)
-    comp(1, 1)
-    ring_step(2, 1)
-    spread(3)
-    relay(2)
-    ring_step(2, 2)
-    wait_swap(4)
-    ring_step(3, 0)
-    ring_step(2, 3)
     last(2)
-    for d in (0, 1, -1, 2):
-        sibs[2, d].wait_recv()
-    comp(2, 0)
-    comp(2, 1)
     ring_end(2)
-    comp(2, 2)
     comp(1, 2)
     comp(0, 2)
-    ring_step(3, 1)
-    relay(3)
-    for d in (0, 1, -1):
-        sibs[3, d].wait_recv()
-        comp_slab(3, d)
-    ring_step(3, 2)
+    wait_sib(2)
+    comp(2, 0)
     last(3)
+    fold(0, 1)
+    fold(2, 0)
+    ring_half(3, 1, 0)
+    comp(2, 1)
+    fold(2, 1)
+    comp(2, 2)
+    sibs[3, -1].wait_recv()
+    comp_slab(3, -1)
+    fold(0, 2)
+    ring_half(3, 1, 1)
+    sibs[3, 0].wait_recv()
+    comp_slab(3, 0)
+    fold(2, 2)
+    sibs[3, 1].wait_recv()
+    comp_slab(3, 1)
     sibs[3, 2].wait_recv()
     comp_slab(3, 2)
-    ring_step(3, 3)
+    ring_half(3, 2, 0)
+    fold(1, 0)
+    ring_half(3, 2, 1)
+    fold(1, 1)
+    fold(1, 2)
+    ring_half(3, 3, 0)
+    fold(3, -1)
+    fold(3, 0)
+    fold(3, 1)
+    fold(3, 2)
+    ring_half(3, 3, 1)
 
     def rotate(u):
         return (u * cos_b + pltpu.roll(u, 64, axis=1) * sin_b).astype(BF)
 
-    for slot in range(3):
+    start, cos, sin = tab["start"], tab["cos"], tab["sin"]
+    for slot in range(2):
         pltpu.make_async_copy(got.at[slot], got.at[slot], got_sem.at[slot]).wait()
     for b in (0, 1):
         r = SLOT[(0, b)]
@@ -334,9 +422,10 @@
         sin_b = jnp.where(half == 0, sin[0:256], sin[256:512])
         for i in range(6):
             cols = slice(i * 128, (i + 1) * 128)
-            u = part[r, yl, :, cols].astype(F32)
-            for slot in range(3):
-                u += got[slot, rows_b, cols].astype(F32)
+            u = part[r, yl, :, :, cols].astype(F32)
+            for slot in range(2):
+                u += got[slot, half, :, :, cols].astype(F32)
+            u = u.reshape(256, 128)
             if i == 0:
                 ks[rows_b, :] = rotate(u)
             elif i == 1:
@@ -364,36 +453,35 @@
 
     order = ((2, 0), (2, 1), (1, 0), (3, 0), (1, 1), (3, 1), (0, 0), (0, 1))
 
-    def mixed_refs(n):
-        d, l = order[n]
+    def mixed_refs(n, r):
+        d, f = order[n]
         xx = (x + d) % 4
+        l = flip(flip(yl, RELS[r][1]), f)
         return mixed.at[l, xx], m.at[yh, l, xx, :, at(k * 512, 512)]
 
     def mixed_sib(n):
-        src, dst = mixed_refs(n)
+        src, dst = mixed_refs(n, 0)
         return pltpu.make_async_remote_copy(
             src_ref=src, dst_ref=dst, send_sem=m_send.at[n], recv_sem=m_recv.at[n, yh, k],
             device_id=sib, device_id_type=MESH)
 
     def send_mixed(n):
-        src, dst = mixed_refs(n)
         for r in (2, 1, 3):
+            src, dst = mixed_refs(n, r)
             cps.go(src, dst, mdev(RELS[r]), recv=m_recv.at[n, yh, k])
 
         @pl.when(k == yl)
         def _():
+            src, dst = mixed_refs(n, 0)
             pltpu.make_async_copy(src, dst, m_recv.at[n, yh, k]).start()
 
         @pl.when(k != yl)
         def _():
             mixed_sib(n).start()
 
-    attend(0)
-    attend(1)
-    send_mixed(0)
-    attend(2)
-    attend(3)
-    for n in range(1, 8):
+    for i in range(4):
+        attend(i)
+    for n in range(8):
         send_mixed(n)
     ring_end(3)
     for cp in shared:
@@ -402,7 +490,8 @@
     lo_cols, hi_cols = pl.ds(0, 1024), pl.ds(1024, 1024)
 
     def comp_out(n):
-        d, l = order[n]
+        d, f = order[n]
+        l = flip(yl, f)
         xx = (x + d) % 4
         for a in (0, 1):
             for j in (0, 1):
@@ -415,15 +504,10 @@
             part2[d, :, l, :, at(zz * 256, 256)] = o.reshape(2, 64, 256)
             return carry
         lax.fori_loop(0, 8, one, 0)
-
-    for n in (0, 1):
-        comp_out(n)
-        l = order[n][1]
-        for a in (0, 1):
-            cps.go(part2.at[2, a, l, :, hi_cols], fwd.at[0, a, l], xdev(1), recv=fwd_sem.at[0, a, l])
-            cps.go(part2.at[2, a, l, :, lo_cols], fwd.at[1, a, l], xdev(-1), recv=fwd_sem.at[1, a, l])
-    for n in range(2, 6):
-        comp_out(n)
+        if d == 2:
+            for a in (0, 1):
+                cps.go(part2.at[2, a, l, :, hi_cols], fwd.at[0, a, l], xdev(1), recv=fwd_sem.at[0, a, l])
+                cps.go(part2.at[2, a, l, :, lo_cols], fwd.at[1, a, l], xdev(-1), recv=fwd_sem.at[1, a, l])
 
     alone, summed = {}, {}
     rel_order = (2, 1, 3, 0)
@@ -431,7 +515,7 @@
     def slab_at(r):
         return flip(yh, RELS[r][0]), flip(yl, RELS[r][1])
 
-    for r in rel_order:
+    def send_slab(r):
         a, l = slab_at(r)
         alone[r, 1] = cps.go(part2.at[1, a, l, :, lo_cols], rx.at[0, r, :, lo_cols], xdev(1))
         alone[r, -1] = cps.go(part2.at[3, a, l, :, hi_cols], rx.at[1, r, :, hi_cols], xdev(-1))
@@ -442,6 +526,14 @@
                 part2[d % 4, a, l, :, cols].astype(F32) + fwd[i, a, l].astype(F32)).astype(BF)
             pcols = pl.ds(cols.start, 1024)
             summed[r, d] = cps.go(part2.at[d % 4, a, l, :, pcols], rx.at[i, r, :, pcols], xdev(d))
+
+    for n in range(4):
+        comp_out(n)
+    send_slab(2)
+    for n in range(4, 6):
+        comp_out(n)
+    for r in (1, 3, 0):
+        send_slab(r)
     for n in (6, 7):
         comp_out(n)
 
@@ -490,8 +582,10 @@
             pltpu.VMEM((4, 2, 4, 64, 2048), BF),
             pltpu.VMEM((3, 2048, 256), BF),
             pltpu.VMEM((8, 1024, 256), BF),
-            pltpu.VMEM((4, 2, 256, 768), BF),
-            pltpu.VMEM((3, 512, 768), BF),
+            pltpu.VMEM((4, 2, 4, 64, 768), BF),
+            pltpu.VMEM((2, 2, 4, 64, 768), BF),
+            pltpu.VMEM((2, 4, 32, 768), BF),
+            pltpu.VMEM((2, 4, 32, 768), BF),
             pltpu.VMEM((2, 8, 512), F32),
             pltpu.VMEM((512, 512), BF),
             pltpu.VMEM((512, 128), BF),
@@ -503,7 +597,7 @@
             pltpu.VMEM((2, 4, 64, 2048), BF),
             pltpu.VMEM((3, 64, 2048), BF),
             pltpu.VMEM((3, 64, 2048), BF),
-            DMA((N_COPIES,)), DMA((N_COPIES,)), DMA, DMA((5,)), DMA((5,)), DMA((3,)),
+            DMA((N_COPIES,)), DMA((N_COPIES,)), DMA, DMA((5,)), DMA((5,)), DMA((2,)),
             DMA((8,)), DMA((8, 2, 2)), DMA((2, 2, 2)),
         ],
         compiler_params=pltpu.CompilerParams(

time: 140 us -> 122 us (0.87); the launches traced: 138 us -> 122 us
  Pallas kernels: 136 us -> 120 us
    pallas_call x1, Pallas kernels: 136 us -> 120 us  [body(): pl.pallas_call(kernel, out_shape=jax.ShapeDtypeStruct((64, 8192), BF), in...]
where the time goes in v3:
time: 122 us
  Pallas kernels  120 us (98%)
  local copies, waits for them, and re-layouts  2.26 us (2%)
    pallas_call x1, Pallas kernels, body(): pl.pallas_call(kernel, out_shape=jax.ShapeDtypeStruct((64, 8192), BF), in...  120 us

profile of v3, /device:TPU:1, one launch (start us, length us, event | category | flops | bytes accessed | tf_op | source)
XLA Modules:
  0.0 122.1 jit_solution(17408614732369757470)
XLA Ops:
  0.0 119.9 %sublayer.1 = bf16[64,8192]{1,0:T(8,128)(2,1)} custom-call(bf16[64,8192]{1,0:T(8,128)(2,1)} %hid_in.1, f32[1,8192]{1,0:T(1,128)} %bitcast.1, s32[1,512]{1,0:T(1,128)} %seg.1, bf16[256,512]{1,0:T(8,128)(2,1)} %wq.1, bf16[256,128]{1,0:T(8,128)(2,1)} %wk.1, bf16[256,128]{1,0:T(8,128)(2,1)} %wv.1, bf16[512,256]{1,0:T(8,128)(2,1)} %wo_in.1), custom_call_target="tpu_custom_call" | custom-call | tf_op jit(solution)/shard_map/sublayer/pallas_call | solution.py:574
  119.9 2.3 %copy.9 = bf16[64,8192]{1,0:T(8,128)(2,1)} copy(bf16[64,8192]{1,0:T(8,128)(2,1)} %sublayer.1) | data formatting | bytes 2097152

commit v4 on v3

--- a/solution.py
+++ b/solution.py
@@ -15,7 +15,6 @@
 
 RELS = ((0, 0), (1, 1), (1, 0), (0, 1))
 SLOT = {r: i for i, r in enumerate(RELS)}
-N_COPIES = 240
 
 
 def place():
@@ -36,34 +35,27 @@
     return pl.ds(pl.multiple_of(start, size), size)
 
 
-class Copies:
-    def __init__(self, send, recv):
-        self.send, self.recv, self.n, self.open = send, recv, 0, []
-
-    def go(self, src, dst, dev, recv=None):
-        i = self.n
-        self.n += 1
-        cp = pltpu.make_async_remote_copy(
-            src_ref=src, dst_ref=dst, send_sem=self.send.at[i],
-            recv_sem=self.recv.at[i] if recv is None else recv,
-            device_id=dev, device_id_type=MESH)
-        cp.start()
-        self.open.append(cp)
-        return cp
-
-    def finish(self):
-        for cp in self.open:
-            cp.wait_send()
+SENDS = ("ring0", "ring1", "ring2", "ring3", "spread", "relay", "sib", "slice", "seg", "far0", "far1", "sum0", "sum1",
+         "mixed1", "mixed2", "mixed3", "share", "fwd", "cross", "last")
+
+
+def wait(ref, sem):
+    pltpu.make_async_copy(ref, ref, sem).wait()
 
 
 def kernel(hid_in, gain, seg, wq, wk, wv, wo_in, out,
-           hid, xn, xs, w, wo, part, got, fa, fb, segs, qs, ks, vs, mixed, m, part2, fwd, rx, slab, ry,
-           send, recv, hid_sem, swap_send, swap_recv, got_sem, m_send, m_recv, fwd_sem):
+           hid, xn, xs, w, wo, part, got, fa, fb, segs, qs, ks, vs, mixed, m, part2, fwd, rx, slab,
+           send, hid_sem, seg_sem, swap_send, swap_recv, y_recv, xg_recv, xh_recv, sib_recv, last_sib_recv,
+           ring_recv, far_recv, share_recv, got_recv, m_send, m_recv, fwd_recv, cross_recv, last_recv):
     x, yh, yl, z, k = place()
     y_self = yh * 2 + yl
     sib = device(x, yh, yl, z, 1 - k)
     swapped = device(x, yh, k, z, yl)
-    cps = Copies(send, recv)
+
+    def go(name, src, dst, dev, recv):
+        pltpu.make_async_remote_copy(
+            src_ref=src, dst_ref=dst, send_sem=send.at[SENDS.index(name)], recv_sem=recv,
+            device_id=dev, device_id_type=MESH).start()
 
     def ydev(r):
         return device(x, flip(yh, r[0]), flip(yl, r[1]), z, k)
@@ -109,34 +101,25 @@
     wo_mine = wo.at[z, at(k * 512, 512), :]
     wo_theirs = wo.at[z, at(yl * 512, 512), :]
 
-    def swap_copy(i):
-        src, dst = pieces[i] if i < 4 else (wo_in, wo_theirs)
-        return pltpu.make_async_remote_copy(
-            src_ref=src, dst_ref=dst, send_sem=swap_send.at[i], recv_sem=swap_recv.at[i],
-            device_id=swapped, device_id_type=MESH)
-
-    def own_copy(i):
-        src, dst = pieces[i] if i < 4 else (wo_in, wo_mine)
-        return pltpu.make_async_copy(src, dst, swap_recv.at[i])
-
     groups = ((0, 1), (2,), (3,), (4,))
 
     def swap(group):
-        which = groups[group]
-
         @pl.when(k != yl)
         def _():
-            for i in which:
-                swap_copy(i).start()
+            for i in groups[group]:
+                src, dst = pieces[i] if i < 4 else (wo_in, wo_theirs)
+                pltpu.make_async_remote_copy(
+                    src_ref=src, dst_ref=dst, send_sem=swap_send, recv_sem=swap_recv.at[group],
+                    device_id=swapped, device_id_type=MESH).start()
 
         @pl.when(k == yl)
         def _():
-            for i in which:
-                own_copy(i).start()
+            for i in groups[group]:
+                src, dst = pieces[i] if i < 4 else (wo_in, wo_mine)
+                pltpu.make_async_copy(src, dst, swap_recv.at[group]).start()
 
     def wait_swap(group):
-        for i in groups[group]:
-            own_copy(i).wait()
+        wait(w.at[group, rows, :] if group < 3 else wo_mine, swap_recv.at[group])
 
     swap(0)
 
@@ -161,76 +144,77 @@
             xn[r - 1, :, zz * 256:(zz + 1) * 256] = v
         slice_norm(RELS[r], put)
 
-    xg, xh, sibs, ysend = {}, {}, {}, {}
+    slab_ref = xs.at[0, 0, 0]
 
     def to_sib(r, d):
         ref = xs.at[r, k, (x - d + 4) % 4]
-        sibs[r, d] = cps.go(ref, ref, sib)
+        go("sib", ref, ref, sib, sib_recv.at[r] if r < 3 else last_sib_recv.at[d % 4])
+
+    def wait_sib(r):
+        wait(xs.at[r, 1 - k], sib_recv.at[r])
+
+    def wait_last_sib(d):
+        wait(slab_ref, last_sib_recv.at[d % 4])
 
     def spread(r):
         if r:
-            ysend[r].wait_recv()
+            wait(slab_ref, y_recv.at[r - 1])
         ref = xs.at[r, k, x]
-        for d in (1, -1):
-            xg[r, d] = cps.go(ref, ref, xdev(d))
+        for i, d in enumerate((1, -1)):
+            go("spread", ref, ref, xdev(d), xg_recv.at[r, i])
         to_sib(r, 0)
 
     def relay(r, d):
-        xg[r, d].wait_recv()
+        wait(slab_ref, xg_recv.at[r, 0 if d == 1 else 1])
         ref = xs.at[r, k, (x - d + 4) % 4, pl.ds(0 if d == 1 else 32, 32)]
-        xh[r, d] = cps.go(ref, ref, xdev(d))
+        go("relay", ref, ref, xdev(d), xh_recv.at[r])
         to_sib(r, d)
 
     def last(r):
-        xh[r, 1].wait_recv()
-        xh[r, -1].wait_recv()
+        wait(slab_ref, xh_recv.at[r])
         to_sib(r, 2)
-
-    ring = {}
 
     def ring_ref(n, b, hf):
         if n < 3:
             return w.at[n, at(b * 256 + hf * 128, 128), :]
         return wo.at[b, at(k * 512 + hf * 256, 256), :]
 
+    def ring_wait(n, i):
+        wait(w.at[n, pl.ds(0, 256), :] if n < 3 else wo.at[0, pl.ds(0, 512), :], ring_recv.at[n, i])
+
     def share(b):
         ref = wo.at[b, at(k * 512, 512), :]
-        shared.append(cps.go(ref, ref, sib))
-
-    shared = []
+        go("share", ref, ref, sib, share_recv)
 
     def ring_half(n, s, hf):
+        if s > 0:
+            ring_wait(n, s * 2 - 2 + hf)
         for d in (1, -1):
-            if s > 0:
-                ring[n, s - 1, hf, d].wait_recv()
             if s == 3 and hf != (0 if d == 1 else 1):
                 continue
             ref = ring_ref(n, (z - d * s + 8) % 8, hf)
-            ring[n, s, hf, d] = cps.go(ref, ref, zdev(d))
+            go("ring%d" % n, ref, ref, zdev(d), ring_recv.at[n, min(s * 2 + hf, 6)])
         if n == 3 and hf == 1:
             share((z + s) % 8)
             if s:
                 share((z - s + 8) % 8)
 
-    def ring_step(n, s):
-        ring_half(n, s, 0)
-        ring_half(n, s, 1)
-
     def ring_end(n):
-        ring[n, 3, 0, 1].wait_recv()
-        ring[n, 3, 1, -1].wait_recv()
+        ring_wait(n, 6)
         if n == 3:
             share((z + 4) % 8)
 
-    far_a, far_b = {}, {}
     near, pair = RELS[1], RELS[3]
     low, high = pl.ds(0, 32), pl.ds(32, 32)
 
     def send_sum(r, xx, half, cols):
         a, b = RELS[r]
         slot = 0 if a else 1
-        cps.go(part.at[r, 1 - yl, xx, half, cols], got.at[slot, flip(yl, b), xx, half, cols],
-               ydev(near if a else pair), recv=got_sem.at[slot])
+        go("sum%d" % slot, part.at[r, 1 - yl, xx, half, cols], got.at[slot, flip(yl, b), xx, half, cols],
+           ydev(near if a else pair), got_recv.at[slot])
+
+    def far_sem(i, b, g):
+        return i * 6 + b * 3 + (0 if i and b else g)
 
     def comp(r, g):
         a, b = RELS[r]
@@ -242,8 +226,8 @@
             return carry
         lax.fori_loop(0, 2, one, 0)
         if a:
-            far_a[b, g] = cps.go(part.at[r, yl, :, low, cols], fa.at[1 - b, :, :, cols], ydev(pair))
-            far_b[b, g] = cps.go(part.at[r, yl, :, high, cols], fb.at[1 - b, :, :, cols], ydev(near))
+            go("far0", part.at[r, yl, :, low, cols], fa.at[1 - b, :, :, cols], ydev(pair), far_recv.at[far_sem(0, 1 - b, g)])
+            go("far1", part.at[r, yl, :, high, cols], fb.at[1 - b, :, :, cols], ydev(near), far_recv.at[far_sem(1, 1 - b, g)])
             send_sum(r, slice(None), high, cols)
         else:
             send_sum(r, slice(None), low, cols)
@@ -263,12 +247,13 @@
 
     def fold(r, i):
         a, b = RELS[r]
-        far, buf, half, rows32 = (far_a, fa, low, slice(0, 32)) if a else (far_b, fb, high, slice(32, 64))
+        side, buf, half, rows32 = (0, fa, low, slice(0, 32)) if a else (1, fb, high, slice(32, 64))
         slabs = r == 3
-        for g in range(3) if slabs else (i,):
-            if (r, g) not in folded:
-                folded.add((r, g))
-                far[1 - b, g].wait_recv()
+        if not slabs:
+            wait(buf.at[b, :, :, pl.ds(i * 256, 256)], far_recv.at[far_sem(side, b, i)])
+        elif r not in folded:
+            folded.add(r)
+            wait(buf.at[b], far_recv.at[far_sem(side, b, 0)])
         if slabs:
             xx, cols = (x - i + 4) % 4, slice(0, 768)
             part[r, 1 - yl, xx, rows32, cols] = (
@@ -281,16 +266,12 @@
             send_sum(r, slice(None), half, pl.ds(i * 256, 256))
 
     def send_slice(r):
-        ysend[r] = cps.go(xn.at[r - 1], xs.at[r, k, x], ydev(RELS[r]))
-
-    def wait_sib(r):
-        for d in (0, 1, -1, 2):
-            sibs[r, d].wait_recv()
+        go("slice", xn.at[r - 1], xs.at[r, k, x], ydev(RELS[r]), y_recv.at[r - 1])
 
     tab = {}
 
     def tables():
-        seg_cp.wait_recv()
+        wait(segs.at[1], seg_sem)
         own_row = jnp.where(k == yl, segs[0, 0:1, :], segs[1, 0:1, :])
         i_col = lax.broadcasted_iota(jnp.int32, (512, 512), 0)
         i_row = lax.broadcasted_iota(jnp.int32, (512, 512), 1)
@@ -313,7 +294,7 @@
     put_norm(2)
     put_norm(3)
     segs[0] = jnp.broadcast_to(seg[...].astype(F32), (8, 512))
-    seg_cp = cps.go(segs.at[0], segs.at[1], sib)
+    go("seg", segs.at[0], segs.at[1], sib, seg_sem)
 
     wait_swap(0)
     ring_half(0, 0, 0)
@@ -385,16 +366,16 @@
     comp(2, 1)
     fold(2, 1)
     comp(2, 2)
-    sibs[3, -1].wait_recv()
+    wait_last_sib(-1)
     comp_slab(3, -1)
     fold(0, 2)
     ring_half(3, 1, 1)
-    sibs[3, 0].wait_recv()
+    wait_last_sib(0)
     comp_slab(3, 0)
     fold(2, 2)
-    sibs[3, 1].wait_recv()
+    wait_last_sib(1)
     comp_slab(3, 1)
-    sibs[3, 2].wait_recv()
+    wait_last_sib(2)
     comp_slab(3, 2)
     ring_half(3, 2, 0)
     fold(1, 0)
@@ -413,7 +394,7 @@
 
     start, cos, sin = tab["start"], tab["cos"], tab["sin"]
     for slot in range(2):
-        pltpu.make_async_copy(got.at[slot], got.at[slot], got_sem.at[slot]).wait()
+        wait(got.at[slot], got_recv.at[slot])
     for b in (0, 1):
         r = SLOT[(0, b)]
         half = flip(yl, b)
@@ -451,118 +432,132 @@
                 mixed[i // 2, (i % 2) * 2 + half, :, j * 128:(j + 1) * 128] = (
                     o[j * 128 + half * 64:j * 128 + half * 64 + 64])
 
-    order = ((2, 0), (2, 1), (1, 0), (3, 0), (1, 1), (3, 1), (0, 0), (0, 1))
+    order = ((2, 0, 0, 32), (2, 0, 32, 32), (2, 1, 0, 64), (1, 0, 0, 64), (3, 0, 0, 64),
+             (1, 1, 0, 64), (3, 1, 0, 64), (0, 0, 0, 64), (0, 1, 0, 64))
 
     def mixed_refs(n, r):
-        d, f = order[n]
+        d, f, first, size = order[n]
         xx = (x + d) % 4
         l = flip(flip(yl, RELS[r][1]), f)
-        return mixed.at[l, xx], m.at[yh, l, xx, :, at(k * 512, 512)]
-
-    def mixed_sib(n):
-        src, dst = mixed_refs(n, 0)
-        return pltpu.make_async_remote_copy(
-            src_ref=src, dst_ref=dst, send_sem=m_send.at[n], recv_sem=m_recv.at[n, yh, k],
-            device_id=sib, device_id_type=MESH)
+        ps = pl.ds(first, size)
+        return mixed.at[l, xx, ps], m.at[yh, l, xx, ps, at(k * 512, 512)]
 
     def send_mixed(n):
         for r in (2, 1, 3):
             src, dst = mixed_refs(n, r)
-            cps.go(src, dst, mdev(RELS[r]), recv=m_recv.at[n, yh, k])
+            go("mixed%d" % r, src, dst, mdev(RELS[r]), m_recv.at[n])
+        src, dst = mixed_refs(n, 0)
 
         @pl.when(k == yl)
         def _():
-            src, dst = mixed_refs(n, 0)
-            pltpu.make_async_copy(src, dst, m_recv.at[n, yh, k]).start()
+            pltpu.make_async_copy(src, dst, m_recv.at[n]).start()
 
         @pl.when(k != yl)
         def _():
-            mixed_sib(n).start()
+            pltpu.make_async_remote_copy(
+                src_ref=src, dst_ref=dst, send_sem=m_send, recv_sem=m_recv.at[n],
+                device_id=sib, device_id_type=MESH).start()
 
     for i in range(4):
         attend(i)
-    for n in range(8):
+    for n in range(len(order)):
         send_mixed(n)
     ring_end(3)
-    for cp in shared:
-        cp.wait_recv()
+    wait(wo.at[:, pl.ds(0, 512), :], share_recv)
 
     lo_cols, hi_cols = pl.ds(0, 1024), pl.ds(1024, 1024)
 
     def comp_out(n):
-        d, f = order[n]
+        d, f, first, size = order[n]
         l = flip(yl, f)
         xx = (x + d) % 4
-        for a in (0, 1):
-            for j in (0, 1):
-                ref = m.at[a, l, xx, :, pl.ds(j * 512, 512)]
-                pltpu.make_async_copy(ref, ref, m_recv.at[n, a, j]).wait()
-        lhs = m[:, l, xx].reshape(128, 1024)
-
-        def one(zz, carry):
-            o = jnp.dot(lhs, wo[zz], preferred_element_type=F32).astype(BF)
-            part2[d, :, l, :, at(zz * 256, 256)] = o.reshape(2, 64, 256)
-            return carry
-        lax.fori_loop(0, 8, one, 0)
-        if d == 2:
-            for a in (0, 1):
-                cps.go(part2.at[2, a, l, :, hi_cols], fwd.at[0, a, l], xdev(1), recv=fwd_sem.at[0, a, l])
-                cps.go(part2.at[2, a, l, :, lo_cols], fwd.at[1, a, l], xdev(-1), recv=fwd_sem.at[1, a, l])
-
-    alone, summed = {}, {}
+        ps = pl.ds(first, size)
+        wait(m.at[:, l, xx, ps], m_recv.at[n])
+        lhs = m[:, l, xx, first:first + size].reshape(2 * size, 1024)
+
+        def some(lo, count):
+            def one(i, carry):
+                zz = lo + i
+                o = jnp.dot(lhs, wo[zz], preferred_element_type=F32).astype(BF)
+                part2[d, :, l, first:first + size, at(zz * 256, 256)] = o.reshape(2, size, 256)
+                return carry
+            lax.fori_loop(0, count, one, 0)
+            if d == 2:
+                i = 0 if lo >= 4 else 1
+                go("fwd", part2.at[2, :, l, ps, pl.ds(lo * 256, count * 256)],
+                   fwd.at[i, :, l, ps, pl.ds(lo % 4 * 256, count * 256)], xdev(1 if lo >= 4 else -1), fwd_recv.at[i, l])
+
+        if n == 0:
+            for lo in (4, 0, 6, 2):
+                some(lo, 2)
+        elif d == 2:
+            some(4, 4)
+            some(0, 4)
+        else:
+            some(0, 8)
+
     rel_order = (2, 1, 3, 0)
 
     def slab_at(r):
         return flip(yh, RELS[r][0]), flip(yl, RELS[r][1])
 
-    def send_slab(r):
+    def parts_of(r):
+        return (slice(0, 32), slice(32, 64)) if r == 3 else (slice(0, 64),)
+
+    def cross_sem(r, p):
+        return cross_recv.at[r + p.start // 32]
+
+    def send_side(r, d):
         a, l = slab_at(r)
-        alone[r, 1] = cps.go(part2.at[1, a, l, :, lo_cols], rx.at[0, r, :, lo_cols], xdev(1))
-        alone[r, -1] = cps.go(part2.at[3, a, l, :, hi_cols], rx.at[1, r, :, hi_cols], xdev(-1))
-        for i, d, cols in ((0, 1, slice(1024, 2048)), (1, -1, slice(0, 1024))):
-            ref = fwd.at[i, a, l]
-            pltpu.make_async_copy(ref, ref, fwd_sem.at[i, a, l]).wait()
-            part2[d % 4, a, l, :, cols] = (
-                part2[d % 4, a, l, :, cols].astype(F32) + fwd[i, a, l].astype(F32)).astype(BF)
-            pcols = pl.ds(cols.start, 1024)
-            summed[r, d] = cps.go(part2.at[d % 4, a, l, :, pcols], rx.at[i, r, :, pcols], xdev(d))
-
-    for n in range(4):
+        i, plain, cols = (0, lo_cols, slice(1024, 2048)) if d == 1 else (1, hi_cols, slice(0, 1024))
+        pcols = pl.ds(cols.start, 1024)
+        if r in (2, 1):
+            wait(fwd.at[i, :, l], fwd_recv.at[i, l])
+        for p in parts_of(r):
+            ps = pl.ds(p.start, p.stop - p.start)
+            go("cross", part2.at[d % 4, a, l, ps, plain], rx.at[i, r, ps, plain], xdev(d), cross_sem(r, p))
+            part2[d % 4, a, l, p, cols] = (
+                part2[d % 4, a, l, p, cols].astype(F32) + fwd[i, a, l, p].astype(F32)).astype(BF)
+            go("cross", part2.at[d % 4, a, l, ps, pcols], rx.at[i, r, ps, pcols], xdev(d), cross_sem(r, p))
+
+    for n in range(3):
         comp_out(n)
-    send_slab(2)
-    for n in range(4, 6):
+    for n, r, d in ((3, 2, 1), (4, 2, -1), (5, 1, 1), (6, 1, -1)):
         comp_out(n)
-    for r in (1, 3, 0):
-        send_slab(r)
-    for n in (6, 7):
+        send_side(r, d)
+    for r in (3, 0):
+        for d in (1, -1):
+            send_side(r, d)
+    for n in (7, 8):
         comp_out(n)
 
-    last_send = {}
     for r in rel_order:
         a, l = slab_at(r)
-        for d in (1, -1):
-            alone[r, d].wait_recv()
-            summed[r, d].wait_recv()
-        o = (part2[0, a, l].astype(F32) + rx[0, r].astype(F32) + rx[1, r].astype(F32)).astype(BF)
-        if r:
-            slab[r - 1] = o
-            last_send[r] = cps.go(slab.at[r - 1], ry.at[r - 1], ydev(RELS[r]))
-        else:
-            for zz in range(8):
-                out[:, at((zz * 4 + y_self) * 256, 256)] = o[:, zz * 256:(zz + 1) * 256]
+        for p in parts_of(r):
+            ps = pl.ds(p.start, p.stop - p.start)
+            wait(rx.at[:, r, ps], cross_sem(r, p))
+            o = (part2[0, a, l, p].astype(F32) + rx[0, r, p].astype(F32) + rx[1, r, p].astype(F32)).astype(BF)
+            if r:
+                slab[r - 1, p] = o
+                go("last", slab.at[r - 1, ps], out.at[y_self, ps], ydev(RELS[r]), last_recv.at[r - 1])
+            else:
+                out[y_self] = o
     for r in (2, 1, 3):
-        a, l = slab_at(r)
-        last_send[r].wait_recv()
-        for zz in range(8):
-            out[:, at((zz * 4 + a * 2 + l) * 256, 256)] = ry[r - 1, :, zz * 256:(zz + 1) * 256]
+        wait(slab.at[r - 1], last_recv.at[r - 1])
 
     @pl.when(k != yl)
     def _():
-        for i in range(5):
-            swap_copy(i).wait_send()
-        for n in range(8):
-            mixed_sib(n).wait_send()
-    cps.finish()
+        wait(w.at[0, pl.ds(0, 1280), :], swap_send)
+        wait(mixed, m_send)
+
+    sent = dict(
+        ring3=w.at[pl.ds(0, 2), pl.ds(0, 1792), :], spread=xs.at[0], relay=xs.at[0, 0], sib=xs.at[pl.ds(0, 2)], slice=xn,
+        seg=segs.at[0], far0=fa, far1=fb, sum0=got.at[0], sum1=got.at[1], mixed1=mixed, mixed2=mixed, mixed3=mixed,
+        share=wo.at[:, pl.ds(0, 512), :], fwd=fwd, cross=rx, last=slab)
+    for n in range(3):
+        sent["ring%d" % n] = w.at[n, pl.ds(0, 1792), :]
+    for i, name in enumerate(SENDS):
+        wait(sent[name], send.at[i])
 
 
 V = pl.BlockSpec(memory_space=pltpu.VMEM)
@@ -570,10 +565,27 @@
 DMA = pltpu.SemaphoreType.DMA
 
 
+def interleave_kernel(blocks, out):
+    for y in range(4):
+        for zz in range(8):
+            out[:, (zz * 4 + y) * 256:(zz * 4 + y + 1) * 256] = blocks[y, :, zz * 256:(zz + 1) * 256]
+
+
+def interleave(blocks):
+    return pl.pallas_call(
+        interleave_kernel,
+        grid=(2,),
+        out_shape=jax.ShapeDtypeStruct((64, 8192), BF),
+        in_specs=[pl.BlockSpec((4, 32, 2048), lambda i: (0, i, 0))],
+        out_specs=pl.BlockSpec((32, 8192), lambda i: (i, 0)),
+        name="interleave",
+    )(blocks)
+
+
 def body(hidden, gain, segment_ids, w_query, key_matrix, value_matrix, w_out):
-    return pl.pallas_call(
+    blocks = pl.pallas_call(
         kernel,
-        out_shape=jax.ShapeDtypeStruct((64, 8192), BF),
+        out_shape=jax.ShapeDtypeStruct((4, 64, 2048), BF),
         in_specs=[ANY, V, V, ANY, ANY, ANY, ANY],
         out_specs=V,
         scratch_shapes=[
@@ -596,14 +608,16 @@
             pltpu.VMEM((2, 2, 2, 64, 1024), BF),
             pltpu.VMEM((2, 4, 64, 2048), BF),
             pltpu.VMEM((3, 64, 2048), BF),
-            pltpu.VMEM((3, 64, 2048), BF),
-            DMA((N_COPIES,)), DMA((N_COPIES,)), DMA, DMA((5,)), DMA((5,)), DMA((2,)),
-            DMA((8,)), DMA((8, 2, 2)), DMA((2, 2, 2)),
+            DMA((len(SENDS),)), DMA, DMA, DMA, DMA((4,)),
+            DMA((3,)), DMA((4, 2)), DMA((4,)), DMA((3,)), DMA((4,)),
+            DMA((4, 7)), DMA((10,)), DMA, DMA((2,)),
+            DMA, DMA((9,)), DMA((2, 2)), DMA((5,)), DMA((3,)),
         ],
         compiler_params=pltpu.CompilerParams(
             collective_id=0, has_side_effects=True, vmem_limit_bytes=VMEM_LIMIT),
         name="sublayer",
     )(hidden, gain.reshape(1, -1), segment_ids, w_query, key_matrix, value_matrix, w_out)
+    return interleave(blocks)
 
 
 def solution(mesh):

time: 122 us -> 116 us (0.951)
  Pallas kernels: 120 us -> 116 us
  local copies, waits for them, and re-layouts: 2.26 us -> 0 us
    pallas_call x1 -> x2, Pallas kernels: 120 us -> 116 us  [the longest x1 114 us: body(): pl.pallas_call(kernel, out_shape=jax.ShapeDtypeStruct((4, 64, 2048), BF),...]
    unnamed x1 -> x0, local copies, waits for them, and re-layouts: 2.26 us -> none
where the time goes in v4:
time: 116 us
  Pallas kernels  116 us (100%)
    pallas_call x1, Pallas kernels, body(): pl.pallas_call(kernel, out_shape=jax.ShapeDtypeStruct((4, 64, 2048), BF),...  114 us

profile of v4, /device:TPU:1, one launch (start us, length us, event | category | flops | bytes accessed | tf_op | source)
XLA Modules:
  0.0 115.7 jit_solution(329720677748219164)
XLA Ops:
  0.0 113.6 %sublayer.1.blocks = bf16[4,64,2048]{2,1,0:T(8,128)(2,1)} custom-call(bf16[64,8192]{1,0:T(8,128)(2,1)} %hid_in.1, f32[1,8192]{1,0:T(1,128)} %bitcast.1, s32[1,512]{1,0:T(1,128)} %seg.1, bf16[256,512]{1,0:T(8,128)(2,1)} %wq.1, bf16[256,128]{1,0:T(8,128)(2,1)} %wk.1, bf16[256,128]{1,0:T(8,128)(2,1)} %wv.1, bf16[512,256]{1,0:T(8,128)(2,1)} %wo_in.1), custom_call_target="tpu_custom_call" | custom-call | tf_op jit(solution)/shard_map/sublayer/pallas_call | solution.py:586
  113.6 2.1 %interleave.1 = bf16[64,8192]{1,0:T(8,128)(2,1)} custom-call(bf16[4,64,2048]{2,1,0:T(8,128)(2,1)} %sublayer.1.blocks), custom_call_target="tpu_custom_call" | custom-call | tf_op jit(solution)/shard_map/interleave/pallas_call | solution.py:575

commit v5 on v4

--- a/solution.py
+++ b/solution.py
@@ -45,7 +45,7 @@
 
 def kernel(hid_in, gain, seg, wq, wk, wv, wo_in, out,
            hid, xn, xs, w, wo, part, got, fa, fb, segs, qs, ks, vs, mixed, m, part2, fwd, rx, slab,
-           send, hid_sem, seg_sem, swap_send, swap_recv, y_recv, xg_recv, xh_recv, sib_recv, last_sib_recv,
+           send, hid_sem, seg_sem, swap_send, swap_recv, y_recv, xg_recv, xh_recv, sib_recv,
            ring_recv, far_recv, share_recv, got_recv, m_send, m_recv, fwd_recv, cross_recv, last_recv):
     x, yh, yl, z, k = place()
     y_self = yh * 2 + yl
@@ -89,6 +89,32 @@
                     pl.semaphore_signal(bar, inc=1, device_id=src, device_id_type=MESH)
             else:
                 pl.semaphore_signal(bar, inc=1, device_id=src, device_id_type=MESH)
+
+    hid_cp.wait()
+    total = jnp.zeros((64, 256), F32)
+    for i in range(32):
+        v = hid[:, i * 256:(i + 1) * 256].astype(F32)
+        total += v * v
+    inv = lax.rsqrt(jnp.sum(total, axis=-1, keepdims=True) * (1.0 / 8192) + 1e-5)
+
+    def slice_norm(r, store):
+        yy = flip(yh, r[0]) * 2 + flip(yl, r[1])
+        for zz in range(8):
+            cols = at((zz * 4 + yy) * 256, 256)
+            store(zz, (hid[:, cols].astype(F32) * inv * gain[:, cols]).astype(BF))
+
+    def put0(zz, v):
+        xs[0, k, x, :, zz * 256:(zz + 1) * 256] = v
+
+    def put_norm(r):
+        def put(zz, v):
+            xn[r - 1, :, zz * 256:(zz + 1) * 256] = v
+        slice_norm(RELS[r], put)
+
+    for r in (1, 2, 3):
+        put_norm(r)
+    slice_norm(RELS[0], put0)
+    segs[0] = jnp.broadcast_to(seg[...].astype(F32), (8, 512))
     pl.semaphore_wait(bar, 11 + 2 * ((k + yl) % 2))
 
     rows = at(z * 256, 256)
@@ -121,40 +147,14 @@
     def wait_swap(group):
         wait(w.at[group, rows, :] if group < 3 else wo_mine, swap_recv.at[group])
 
-    swap(0)
-
-    hid_cp.wait()
-    total = jnp.zeros((64, 256), F32)
-    for i in range(32):
-        v = hid[:, i * 256:(i + 1) * 256].astype(F32)
-        total += v * v
-    inv = lax.rsqrt(jnp.sum(total, axis=-1, keepdims=True) * (1.0 / 8192) + 1e-5)
-
-    def slice_norm(r, store):
-        yy = flip(yh, r[0]) * 2 + flip(yl, r[1])
-        for zz in range(8):
-            cols = at((zz * 4 + yy) * 256, 256)
-            store(zz, (hid[:, cols].astype(F32) * inv * gain[:, cols]).astype(BF))
-
-    def put0(zz, v):
-        xs[0, k, x, :, zz * 256:(zz + 1) * 256] = v
-
-    def put_norm(r):
-        def put(zz, v):
-            xn[r - 1, :, zz * 256:(zz + 1) * 256] = v
-        slice_norm(RELS[r], put)
-
     slab_ref = xs.at[0, 0, 0]
 
     def to_sib(r, d):
         ref = xs.at[r, k, (x - d + 4) % 4]
-        go("sib", ref, ref, sib, sib_recv.at[r] if r < 3 else last_sib_recv.at[d % 4])
+        go("sib", ref, ref, sib, sib_recv.at[r])
 
     def wait_sib(r):
         wait(xs.at[r, 1 - k], sib_recv.at[r])
-
-    def wait_last_sib(d):
-        wait(slab_ref, last_sib_recv.at[d % 4])
 
     def spread(r):
         if r:
@@ -214,7 +214,7 @@
            ydev(near if a else pair), got_recv.at[slot])
 
     def far_sem(i, b, g):
-        return i * 6 + b * 3 + (0 if i and b else g)
+        return i * 6 + b * 3 + g
 
     def comp(r, g):
         a, b = RELS[r]
@@ -232,38 +232,14 @@
         else:
             send_sum(r, slice(None), low, cols)
 
-    def comp_slab(r, d):
-        xx = (x - d + 4) % 4
-        lhs = xs[r, :, xx].reshape(128, 2048)
-
-        def one(g, carry):
-            o = jnp.dot(lhs, w[g], preferred_element_type=F32).astype(BF)
-            part[r, :, xx, :, at(g * 256, 256)] = o.reshape(2, 64, 256)
-            return carry
-        lax.fori_loop(0, 3, one, 0)
-        send_sum(r, xx, low, slice(None))
-
-    folded = set()
-
-    def fold(r, i):
+    def fold(r, g):
         a, b = RELS[r]
         side, buf, half, rows32 = (0, fa, low, slice(0, 32)) if a else (1, fb, high, slice(32, 64))
-        slabs = r == 3
-        if not slabs:
-            wait(buf.at[b, :, :, pl.ds(i * 256, 256)], far_recv.at[far_sem(side, b, i)])
-        elif r not in folded:
-            folded.add(r)
-            wait(buf.at[b], far_recv.at[far_sem(side, b, 0)])
-        if slabs:
-            xx, cols = (x - i + 4) % 4, slice(0, 768)
-            part[r, 1 - yl, xx, rows32, cols] = (
-                part[r, 1 - yl, xx, rows32, cols].astype(F32) + buf[b, xx].astype(F32)).astype(BF)
-            send_sum(r, xx, half, slice(None))
-        else:
-            cols = slice(i * 256, (i + 1) * 256)
-            part[r, 1 - yl, :, rows32, cols] = (
-                part[r, 1 - yl, :, rows32, cols].astype(F32) + buf[b, :, :, cols].astype(F32)).astype(BF)
-            send_sum(r, slice(None), half, pl.ds(i * 256, 256))
+        cols = slice(g * 256, (g + 1) * 256)
+        wait(buf.at[b, :, :, pl.ds(g * 256, 256)], far_recv.at[far_sem(side, b, g)])
+        part[r, 1 - yl, :, rows32, cols] = (
+            part[r, 1 - yl, :, rows32, cols].astype(F32) + buf[b, :, :, cols].astype(F32)).astype(BF)
+        send_sum(r, slice(None), half, pl.ds(g * 256, 256))
 
     def send_slice(r):
         go("slice", xn.at[r - 1], xs.at[r, k, x], ydev(RELS[r]), y_recv.at[r - 1])
@@ -286,14 +262,10 @@
         sin = jnp.where(lane < 64, -1.0, 1.0) * jnp.sin(angles)
         tab.update(start=start, cos=cos, sin=sin)
 
-    put_norm(1)
+    swap(0)
     send_slice(1)
-    slice_norm(RELS[0], put0)
     spread(0)
     swap(1)
-    put_norm(2)
-    put_norm(3)
-    segs[0] = jnp.broadcast_to(seg[...].astype(F32), (8, 512))
     go("seg", segs.at[0], segs.at[1], sib, seg_sem)
 
     wait_swap(0)
@@ -304,10 +276,10 @@
     ring_half(1, 0, 1)
     swap(2)
     ring_half(0, 1, 0)
+    relay(0, -1)
+    relay(0, 1)
     spread(1)
     send_slice(2)
-    relay(0, -1)
-    relay(0, 1)
     ring_half(0, 1, 1)
     wait_swap(2)
     ring_half(2, 0, 0)
@@ -316,78 +288,74 @@
     ring_half(1, 1, 0)
     ring_half(1, 1, 1)
     ring_half(0, 2, 0)
+    last(0)
+    tables()
     ring_half(0, 2, 1)
     ring_half(2, 1, 0)
-    relay(1, -1)
-    relay(1, 1)
     spread(2)
     send_slice(3)
     ring_half(2, 1, 1)
     ring_half(1, 2, 0)
-    last(0)
-    tables()
+    relay(1, -1)
+    relay(1, 1)
     ring_half(1, 2, 1)
     ring_half(0, 3, 0)
-    last(1)
     ring_half(0, 3, 1)
     ring_half(2, 2, 0)
+    relay(2, -1)
+    relay(2, 1)
     spread(3)
     ring_half(2, 2, 1)
     ring_half(1, 3, 0)
-    relay(2, -1)
-    relay(2, 1)
+    last(1)
     ring_half(1, 3, 1)
     wait_sib(1)
     ring_end(0)
     comp(1, 0)
+    ring_half(2, 3, 0)
+    wait_swap(3)
+    ring_half(3, 0, 0)
     wait_sib(0)
     comp(0, 0)
-    ring_half(2, 3, 0)
     ring_half(2, 3, 1)
-    wait_swap(3)
-    ring_half(3, 0, 0)
     ring_half(3, 0, 1)
+    last(2)
+    ring_end(1)
+    comp(1, 1)
+    comp(0, 1)
+    wait_sib(2)
+    comp(2, 0)
     relay(3, -1)
     relay(3, 1)
-    ring_end(1)
-    comp(1, 1)
-    fold(0, 0)
-    comp(0, 1)
-    last(2)
+    comp(2, 1)
+    ring_half(3, 1, 0)
     ring_end(2)
     comp(1, 2)
+    comp(2, 2)
+    ring_half(3, 1, 1)
     comp(0, 2)
-    wait_sib(2)
-    comp(2, 0)
     last(3)
+    fold(1, 0)
+    fold(2, 0)
+    fold(0, 0)
+    ring_half(3, 2, 0)
+    wait_sib(3)
+    comp(3, 0)
+    fold(3, 0)
+    comp(3, 1)
+    fold(1, 1)
+    fold(2, 1)
+    ring_half(3, 2, 1)
+    comp(3, 2)
     fold(0, 1)
-    fold(2, 0)
-    ring_half(3, 1, 0)
-    comp(2, 1)
-    fold(2, 1)
-    comp(2, 2)
-    wait_last_sib(-1)
-    comp_slab(3, -1)
+    fold(3, 1)
+    ring_half(3, 3, 0)
+    fold(1, 2)
+    fold(2, 2)
     fold(0, 2)
-    ring_half(3, 1, 1)
-    wait_last_sib(0)
-    comp_slab(3, 0)
-    fold(2, 2)
-    wait_last_sib(1)
-    comp_slab(3, 1)
-    wait_last_sib(2)
-    comp_slab(3, 2)
-    ring_half(3, 2, 0)
-    fold(1, 0)
-    ring_half(3, 2, 1)
-    fold(1, 1)
-    fold(1, 2)
-    ring_half(3, 3, 0)
-    fold(3, -1)
-    fold(3, 0)
-    fold(3, 1)
     fold(3, 2)
     ring_half(3, 3, 1)
+    ring_end(3)
 
     def rotate(u):
         return (u * cos_b + pltpu.roll(u, 64, axis=1) * sin_b).astype(BF)
@@ -462,7 +430,6 @@
         attend(i)
     for n in range(len(order)):
         send_mixed(n)
-    ring_end(3)
     wait(wo.at[:, pl.ds(0, 512), :], share_recv)
 
     lo_cols, hi_cols = pl.ds(0, 1024), pl.ds(1024, 1024)
@@ -541,8 +508,9 @@
                 slab[r - 1, p] = o
                 go("last", slab.at[r - 1, ps], out.at[y_self, ps], ydev(RELS[r]), last_recv.at[r - 1])
             else:
-                out[y_self] = o
-    for r in (2, 1, 3):
+                slab[3] = o
+                pltpu.make_async_copy(slab.at[3], out.at[y_self], last_recv.at[3]).start()
+    for r in (2, 1, 3, 4):
         wait(slab.at[r - 1], last_recv.at[r - 1])
 
     @pl.when(k != yl)
@@ -553,7 +521,7 @@
     sent = dict(
         ring3=w.at[pl.ds(0, 2), pl.ds(0, 1792), :], spread=xs.at[0], relay=xs.at[0, 0], sib=xs.at[pl.ds(0, 2)], slice=xn,
         seg=segs.at[0], far0=fa, far1=fb, sum0=got.at[0], sum1=got.at[1], mixed1=mixed, mixed2=mixed, mixed3=mixed,
-        share=wo.at[:, pl.ds(0, 512), :], fwd=fwd, cross=rx, last=slab)
+        share=wo.at[:, pl.ds(0, 512), :], fwd=fwd, cross=rx, last=slab.at[pl.ds(0, 3)])
     for n in range(3):
         sent["ring%d" % n] = w.at[n, pl.ds(0, 1792), :]
     for i, name in enumerate(SENDS):
@@ -587,7 +555,7 @@
         kernel,
         out_shape=jax.ShapeDtypeStruct((4, 64, 2048), BF),
         in_specs=[ANY, V, V, ANY, ANY, ANY, ANY],
-        out_specs=V,
+        out_specs=ANY,
         scratch_shapes=[
             pltpu.VMEM((64, 8192), BF),
             pltpu.VMEM((3, 64, 2048), BF),
@@ -607,11 +575,11 @@
             pltpu.VMEM((4, 2, 2, 64, 2048), BF),
             pltpu.VMEM((2, 2, 2, 64, 1024), BF),
             pltpu.VMEM((2, 4, 64, 2048), BF),
-            pltpu.VMEM((3, 64, 2048), BF),
+            pltpu.VMEM((4, 64, 2048), BF),
             DMA((len(SENDS),)), DMA, DMA, DMA, DMA((4,)),
-            DMA((3,)), DMA((4, 2)), DMA((4,)), DMA((3,)), DMA((4,)),
-            DMA((4, 7)), DMA((10,)), DMA, DMA((2,)),
-            DMA, DMA((9,)), DMA((2, 2)), DMA((5,)), DMA((3,)),
+            DMA((3,)), DMA((4, 2)), DMA((4,)), DMA((4,)),
+            DMA((4, 7)), DMA((12,)), DMA, DMA((2,)),
+            DMA, DMA((9,)), DMA((2, 2)), DMA((5,)), DMA((4,)),
         ],
         compiler_params=pltpu.CompilerParams(
             collective_id=0, has_side_effects=True, vmem_limit_bytes=VMEM_LIMIT),

time: 116 us -> 115 us (level)
  no operation moved by 1% of the time
where the time goes in v5:
time: 115 us
  Pallas kernels  115 us (100%)
    pallas_call x1, Pallas kernels, body(): pl.pallas_call(kernel, out_shape=jax.ShapeDtypeStruct((4, 64, 2048), BF),...  113 us

profile of v5, /device:TPU:1, one launch (start us, length us, event | category | flops | bytes accessed | tf_op | source)
XLA Modules:
  0.0 114.8 jit_solution(8034802173399241594)
XLA Ops:
  0.0 112.7 %sublayer.1.blocks = bf16[4,64,2048]{2,1,0:T(8,128)(2,1)} custom-call(bf16[64,8192]{1,0:T(8,128)(2,1)} %hid_in.1, f32[1,8192]{1,0:T(1,128)} %bitcast.1, s32[1,512]{1,0:T(1,128)} %seg.1, bf16[256,512]{1,0:T(8,128)(2,1)} %wq.1, bf16[256,128]{1,0:T(8,128)(2,1)} %wk.1, bf16[256,128]{1,0:T(8,128)(2,1)} %wv.1, bf16[512,256]{1,0:T(8,128)(2,1)} %wo_in.1), custom_call_target="tpu_custom_call" | custom-call | tf_op jit(solution)/shard_map/sublayer/pallas_call | solution.py:554
  112.7 2.1 %interleave.1 = bf16[64,8192]{1,0:T(8,128)(2,1)} custom-call(bf16[4,64,2048]{2,1,0:T(8,128)(2,1)} %sublayer.1.blocks), custom_call_target="tpu_custom_call" | custom-call | tf_op jit(solution)/shard_map/interleave/pallas_call | solution.py:543

commit v6 on v5

--- a/solution.py
+++ b/solution.py
@@ -469,10 +469,10 @@
         return flip(yh, RELS[r][0]), flip(yl, RELS[r][1])
 
     def parts_of(r):
-        return (slice(0, 32), slice(32, 64)) if r == 3 else (slice(0, 64),)
+        return (slice(0, 32), slice(32, 64)) if r in (3, 0) else (slice(0, 64),)
 
     def cross_sem(r, p):
-        return cross_recv.at[r + p.start // 32]
+        return cross_recv.at[r + p.start // 32 * (5 if r == 0 else 1)]
 
     def send_side(r, d):
         a, l = slab_at(r)
@@ -508,8 +508,8 @@
                 slab[r - 1, p] = o
                 go("last", slab.at[r - 1, ps], out.at[y_self, ps], ydev(RELS[r]), last_recv.at[r - 1])
             else:
-                slab[3] = o
-                pltpu.make_async_copy(slab.at[3], out.at[y_self], last_recv.at[3]).start()
+                slab[3, p] = o
+                pltpu.make_async_copy(slab.at[3, ps], out.at[y_self, ps], last_recv.at[3]).start()
     for r in (2, 1, 3, 4):
         wait(slab.at[r - 1], last_recv.at[r - 1])
 
@@ -579,7 +579,7 @@
             DMA((len(SENDS),)), DMA, DMA, DMA, DMA((4,)),
             DMA((3,)), DMA((4, 2)), DMA((4,)), DMA((4,)),
             DMA((4, 7)), DMA((12,)), DMA, DMA((2,)),
-            DMA, DMA((9,)), DMA((2, 2)), DMA((5,)), DMA((4,)),
+            DMA, DMA((9,)), DMA((2, 2)), DMA((6,)), DMA((4,)),
         ],
         compiler_params=pltpu.CompilerParams(
             collective_id=0, has_side_effects=True, vmem_limit_bytes=VMEM_LIMIT),

time: 115 us -> 115 us (level)
  no operation moved by 1% of the time
where the time goes in v6:
time: 115 us
  Pallas kernels  115 us (100%)
    pallas_call x1, Pallas kernels, body(): pl.pallas_call(kernel, out_shape=jax.ShapeDtypeStruct((4, 64, 2048), BF),...  113 us

profile of v6, /device:TPU:1, one launch (start us, length us, event | category | flops | bytes accessed | tf_op | source)
XLA Modules:
  0.0 114.7 jit_solution(7249211520082905471)
XLA Ops:
  0.0 112.6 %sublayer.1.blocks = bf16[4,64,2048]{2,1,0:T(8,128)(2,1)} custom-call(bf16[64,8192]{1,0:T(8,128)(2,1)} %hid_in.1, f32[1,8192]{1,0:T(1,128)} %bitcast.1, s32[1,512]{1,0:T(1,128)} %seg.1, bf16[256,512]{1,0:T(8,128)(2,1)} %wq.1, bf16[256,128]{1,0:T(8,128)(2,1)} %wk.1, bf16[256,128]{1,0:T(8,128)(2,1)} %wv.1, bf16[512,256]{1,0:T(8,128)(2,1)} %wo_in.1), custom_call_target="tpu_custom_call" | custom-call | tf_op jit(solution)/shard_map/sublayer/pallas_call | solution.py:554
  112.6 2.1 %interleave.1 = bf16[64,8192]{1,0:T(8,128)(2,1)} custom-call(bf16[4,64,2048]{2,1,0:T(8,128)(2,1)} %sublayer.1.blocks), custom_call_target="tpu_custom_call" | custom-call | tf_op jit(solution)/shard_map/interleave/pallas_call | solution.py:543

commit v7 on v5

--- a/solution.py
+++ b/solution.py
@@ -115,7 +115,6 @@
         put_norm(r)
     slice_norm(RELS[0], put0)
     segs[0] = jnp.broadcast_to(seg[...].astype(F32), (8, 512))
-    pl.semaphore_wait(bar, 11 + 2 * ((k + yl) % 2))
 
     rows = at(z * 256, 256)
     pieces = [
@@ -137,12 +136,6 @@
                 pltpu.make_async_remote_copy(
                     src_ref=src, dst_ref=dst, send_sem=swap_send, recv_sem=swap_recv.at[group],
                     device_id=swapped, device_id_type=MESH).start()
-
-        @pl.when(k == yl)
-        def _():
-            for i in groups[group]:
-                src, dst = pieces[i] if i < 4 else (wo_in, wo_mine)
-                pltpu.make_async_copy(src, dst, swap_recv.at[group]).start()
 
     def wait_swap(group):
         wait(w.at[group, rows, :] if group < 3 else wo_mine, swap_recv.at[group])
@@ -262,6 +255,14 @@
         sin = jnp.where(lane < 64, -1.0, 1.0) * jnp.sin(angles)
         tab.update(start=start, cos=cos, sin=sin)
 
+    @pl.when(k == yl)
+    def _():
+        for group in range(4):
+            for i in groups[group]:
+                src, dst = pieces[i] if i < 4 else (wo_in, wo_mine)
+                pltpu.make_async_copy(src, dst, swap_recv.at[group]).start()
+
+    pl.semaphore_wait(bar, 11 + 2 * ((k + yl) % 2))
     swap(0)
     send_slice(1)
     spread(0)

time: 115 us -> 115 us (level)
  no operation moved by 1% of the time
where the time goes in v7:
time: 115 us
  Pallas kernels  115 us (100%)
    pallas_call x1, Pallas kernels, body(): pl.pallas_call(kernel, out_shape=jax.ShapeDtypeStruct((4, 64, 2048), BF),...  113 us

profile of v7, /device:TPU:1, one launch (start us, length us, event | category | flops | bytes accessed | tf_op | source)
XLA Modules:
  0.0 114.9 jit_solution(205214941697928112)
XLA Ops:
  0.0 112.8 %sublayer.1.blocks = bf16[4,64,2048]{2,1,0:T(8,128)(2,1)} custom-call(bf16[64,8192]{1,0:T(8,128)(2,1)} %hid_in.1, f32[1,8192]{1,0:T(1,128)} %bitcast.1, s32[1,512]{1,0:T(1,128)} %seg.1, bf16[256,512]{1,0:T(8,128)(2,1)} %wq.1, bf16[256,128]{1,0:T(8,128)(2,1)} %wk.1, bf16[256,128]{1,0:T(8,128)(2,1)} %wv.1, bf16[512,256]{1,0:T(8,128)(2,1)} %wo_in.1), custom_call_target="tpu_custom_call" | custom-call | tf_op jit(solution)/shard_map/sublayer/pallas_call | solution.py:555
  112.8 2.1 %interleave.1 = bf16[64,8192]{1,0:T(8,128)(2,1)} custom-call(bf16[4,64,2048]{2,1,0:T(8,128)(2,1)} %sublayer.1.blocks), custom_call_target="tpu_custom_call" | custom-call | tf_op jit(solution)/shard_map/interleave/pallas_call | solution.py:544
